TPU v7x, 1024 devices: a whole 4x4x32 slice. The times are simulated.
1024 devices in a mesh: hs: 32 (over z_hi, y, x), tok: 32 (over z_lo, core).
Axes of the slice: x: 4, y: 4, z: 32 (z_hi: 2, z_lo: 16; z = z_hi * 16 + z_lo), core: 2. Of those that a mesh axis runs over, the one named last changes fastest.
Arguments:
- queries: bfloat16 [2, 32, 4096, 384], P(None, 'hs', 'tok'), may hold values from -8 to 8
- out_grads: bfloat16 [2, 32, 4096, 384], P(None, 'hs', 'tok'), may hold values from -6 to 6
- kv_cache: bfloat16 [32, 4096, 256], P('hs', 'tok'), may hold values from -8 to 8
- features: bfloat16 [32, 4096, 384], P('hs', 'tok'), may hold values from -6 to 6
- doc_lens: int32 [4, 4], replicated, may hold values from 1 to 2048, as said below
Outputs:
- query_grads: bfloat16 [2, 32, 4096, 384], P(None, 'hs', 'tok')
- cache_grads: bfloat16 [32, 4096, 256], P('hs', 'tok')
- kv_weight_grads: float32 [3072, 2048], P('tok', 'hs')
Inputs may be any that keep to these rules, and one draw needn't show every extreme that they name: `doc_lens`: each row sums to 4096; in every row the longest document has exactly 2048 tokens, is the second or third document, and starts 128 // 4 to 96 positions after the start of a token shard.
All inputs are finite; a program needn't handle non-finite values.
Results may differ from a plain program's by a relative error of at most 0.024.
Values may be sent and summed in bfloat16 or wider, within the bound.
A program may use at most 32 MiB of HBM per device.

v0:
```python
import jax
import jax.numpy as jnp
from jax import lax
from jax.sharding import PartitionSpec as P

KVH = 8
HD = 128


NEG_FILL = -1e30


def from_partner(value, axis, bit):
    mask = 2**bit
    pairs = [(source, source ^ mask) for source in range(lax.axis_size(axis))]
    return lax.ppermute(value, axis, pairs)


def doc_index(doc_ends, positions):
    return jnp.sum((positions[:, None] >= doc_ends[None, :]).astype(jnp.int32), axis=1)


def halve_block(total_sum, upper_bit, which_dim):
    half_width = total_sum.shape[which_dim] // 2
    lower_part = lax.slice_in_dim(total_sum, 0, half_width, axis=which_dim)
    upper_part = lax.slice_in_dim(total_sum, half_width, 2 * half_width, axis=which_dim)
    kept_part = jnp.where(upper_bit == 1, upper_part, lower_part)
    sent_part = jnp.where(upper_bit == 1, lower_part, upper_part)
    return (kept_part, sent_part)


def shards(queries, out_grads, kv_cache, features, doc_lens):
    row_count = queries.shape[2]
    head_columns = queries.shape[3]
    hs_count = lax.axis_size("hs")
    tok_count = lax.axis_size("tok")
    rank_count = min(KVH, hs_count)
    seq_count = hs_count // rank_count
    hs_place = lax.axis_index("hs")
    tok_place = lax.axis_index("tok")
    sequence = hs_place % seq_count
    seq_length = row_count * tok_count
    score_scale = HD ** (-0.5)
    cache_columns = kv_cache.shape[2]
    window = lax.all_gather(kv_cache[0], "tok", axis=0, tiled=True)
    block_rows = min(512, seq_length)
    blocks_used = ((tok_place + 1) * row_count + block_rows - 1) // block_rows
    kv_heads = cache_columns // (2 * HD)
    group_size = head_columns // HD // kv_heads
    lengths = lax.dynamic_index_in_dim(doc_lens, sequence, 0, keepdims=False)
    doc_ends = jnp.cumsum(lengths)
    query_pos = tok_place * row_count + jnp.arange(row_count, dtype=jnp.int32)
    query_doc = doc_index(doc_ends, query_pos)

    def load_block(block_number):
        first_key = block_number * block_rows
        key_block = lax.dynamic_slice_in_dim(window, first_key, block_rows, 0).reshape(
            block_rows, kv_heads, 2, HD
        )
        key_pos = first_key + jnp.arange(block_rows, dtype=jnp.int32)
        allowed = (key_pos[None, :] <= query_pos[:, None]) & (key_pos[None, :] >= 0)
        allowed = allowed & (doc_index(doc_ends, key_pos)[None, :] == query_doc[:, None])
        return (key_block[:, :, 0], key_block[:, :, 1], allowed)

    grads_acc = jnp.zeros((window.shape[0], kv_heads, 2, HD), jnp.float32)
    query_grads = []
    for layer in range(queries.shape[0]):
        query_rows = queries[layer, 0].reshape(row_count, kv_heads, group_size, HD)
        upstream = out_grads[layer, 0].reshape(row_count, kv_heads, group_size, HD)

        def block_scores(key_rows, value_rows):
            scores = (
                jnp.einsum(
                    "tgrd,kgd->grtk", query_rows, key_rows, preferred_element_type=jnp.float32
                )
                * score_scale
            )
            dweights = jnp.einsum(
                "tgrd,kgd->grtk", upstream, value_rows, preferred_element_type=jnp.float32
            )
            return (scores, dweights)

        def stats_step(block_number, state):
            row_top, row_total, row_weighted = state
            key_rows, value_rows, allowed = load_block(block_number)
            scores, dweights = block_scores(key_rows, value_rows)
            top_new = jnp.maximum(row_top, jnp.max(jnp.where(allowed, scores, NEG_FILL), axis=-1))
            factor = jnp.exp(row_top - top_new)
            exp_terms = jnp.where(allowed, jnp.exp(scores - top_new[..., None]), 0.0)
            row_total = row_total * factor + jnp.sum(exp_terms, axis=-1)
            row_weighted = row_weighted * factor + jnp.sum(exp_terms * dweights, axis=-1)
            return (top_new, row_total, row_weighted)

        zero_rows = jnp.zeros((kv_heads, group_size, row_count), jnp.float32)
        start_state = (
            jnp.full((kv_heads, group_size, row_count), NEG_FILL, jnp.float32),
            zero_rows,
            zero_rows,
        )
        row_top, row_total, row_weighted = lax.fori_loop(0, blocks_used, stats_step, start_state)
        row_delta = row_weighted / row_total

        def grad_step(block_number, state):
            dquery_acc, dcache_acc = state
            key_rows, value_rows, allowed = load_block(block_number)
            scores, dweights = block_scores(key_rows, value_rows)
            weights = jnp.where(
                allowed, jnp.exp(scores - row_top[..., None]) / row_total[..., None], 0.0
            )
            dscores = (weights * (dweights - row_delta[..., None])).astype(jnp.bfloat16)
            weights_b = weights.astype(jnp.bfloat16)
            dquery_acc = dquery_acc + score_scale * jnp.einsum(
                "grtk,kgd->tgrd", dscores, key_rows, preferred_element_type=jnp.float32
            )
            key_grads = score_scale * jnp.einsum(
                "grtk,tgrd->kgd", dscores, query_rows, preferred_element_type=jnp.float32
            )
            dvalues = jnp.einsum(
                "grtk,tgrd->kgd", weights_b, upstream, preferred_element_type=jnp.float32
            )
            first_key = block_number * block_rows
            current = lax.dynamic_slice_in_dim(dcache_acc, first_key, block_rows, 0)
            dcache_acc = lax.dynamic_update_slice_in_dim(
                dcache_acc, current + jnp.stack([key_grads, dvalues], axis=2), first_key, 0
            )
            return (dquery_acc, dcache_acc)

        dquery_start = jnp.zeros((row_count, kv_heads, group_size, HD), jnp.float32)
        dquery_acc, grads_acc = lax.fori_loop(0, blocks_used, grad_step, (dquery_start, grads_acc))
        query_grads.append(dquery_acc.reshape(row_count, head_columns).astype(jnp.bfloat16))
    summed = lax.psum_scatter(
        grads_acc.reshape(seq_length, cache_columns).astype(jnp.bfloat16),
        "tok",
        scatter_dimension=0,
        tiled=True,
    )
    full_rows = features[0]
    seq_bits = seq_count.bit_length() - 1
    hs_bits = hs_count.bit_length() - 1
    tok_bits = tok_count.bit_length() - 1
    for bit_number in range(seq_bits, hs_bits):
        partner = from_partner(full_rows, "hs", bit_number)
        upper_bit = hs_place >> bit_number & 1
        full_rows = jnp.where(
            upper_bit == 1,
            jnp.concatenate([partner, full_rows], axis=1),
            jnp.concatenate([full_rows, partner], axis=1),
        )
    partial_grads = jnp.einsum("tf,tc->fc", full_rows, summed, preferred_element_type=jnp.float32)
    joined_place = lax.axis_index(("hs", "tok"))
    halvings = [(tok_bits + bit_number, 1) for bit_number in reversed(range(seq_bits))]
    halvings = halvings + [(bit_number, 0) for bit_number in reversed(range(tok_bits))]
    weight_total = partial_grads
    for bit_number, which_dim in halvings:
        upper_bit = joined_place >> bit_number & 1
        kept_part, sent_part = halve_block(weight_total, upper_bit, which_dim)
        weight_total = kept_part + from_partner(
            sent_part.astype(jnp.bfloat16), ("hs", "tok"), bit_number
        ).astype(sent_part.dtype)
    return (jnp.stack(query_grads)[:, None], summed[None], weight_total)


def solution(mesh):
    placed = (
        P(None, "hs", "tok", None),
        P(None, "hs", "tok", None),
        P("hs", "tok", None),
        P("hs", "tok", None),
        P(),
    )
    return jax.shard_map(
        shards,
        mesh=mesh,
        in_specs=placed,
        out_specs=(P(None, "hs", "tok", None), P("hs", "tok", None), P("tok", "hs")),
        check_vma=False,
    )
```

profile of v0, /device:TPU:1, one launch (start us, length us, event | category | flops | bytes accessed | tf_op | source)
XLA Modules:
  0.0 855.6 jit_solution(10620879516597896767)
XLA Ops:
  12.2 259.0 %all-gather.3.cloned.1.call-done = bf16[1,4096,256]{1,2,0:T(8,128)(2,1)} async-done(((bf16[1,128,256]{1,2,0:T(8,128)(2,1)}), bf16[1,4096,256]{1,2,0:T(8,128)(2,1)}) %all-gather.3.cloned.1.call-update) | async-done | bytes 2097168 | tf_op jit(solution)/shard_map/all_gather | solution.py:45
  271.1 2.3 while.56
  275.6 4.8 while.57
  280.4 2.3 while.58
  282.7 4.8 while.59
  287.6 2.5 convert_element_type.106
  290.0 17.8 %copy.67 = bf16[4096,1,2,128]{3,2,0,1:T(2,128)(2,1)S(1)} copy(bf16[4096,1,2,128]{3,0,2,1:T(8,128)(2,1)S(1)} %convert_element_type.106) | data formatting | bytes 4194304 | tf_op jit(solution)/shard_map/convert_element_type | solution.py:132
  310.4 3.0 collective-permute-start
  313.4 2.3 collective-permute-done
  315.8 4.5 collective-permute-start.1
  320.3 3.4 collective-permute-done.1
  324.6 18.4 %collective-permute-start.2 = (bf16[128,1536]{1,0:T(8,128)(2,1)}, bf16[128,1536]{1,0:T(8,128)(2,1)}, u32[]{:S(2)}, u32[]{:S(2)}) collective-permute-start(bf16[128,1536]{1,0:T(8,128)(2,1)} %maximum_select_fusion.2), channel_id=1, source_target_pairs={{0,512},{32,544},{64,576},{96,608},{128,640},{160,672},{192,704},{... | collective-permute-start | bytes 1179656 | tf_op jit(solution)/shard_map/ppermute | solution.py:16
  343.0 43.7 %collective-permute-done.2 = bf16[128,1536]{1,0:T(8,128)(2,1)} collective-permute-done((bf16[128,1536]{1,0:T(8,128)(2,1)}, bf16[128,1536]{1,0:T(8,128)(2,1)}, u32[]{:S(2)}, u32[]{:S(2)}) %collective-permute-start.2) | collective-permute-done | bytes 393248 | tf_op jit(solution)/shard_map/ppermute | solution.py:16
  386.7 365.6 %reduce-scatter.2.cloned.1.call-done = bf16[128,256]{1,0:T(8,128)(2,1)} async-done(((bf16[4096,256]{1,0:T(8,128)(2,1)}), bf16[128,256]{1,0:T(8,128)(2,1)}) %reduce-scatter.2.cloned.1.call-update) | async-done | bytes 65552 | tf_op jit(solution)/shard_map/reduce_scatter | solution.py:131
  755.3 4.5 collective-permute-start.3
  759.9 10.0 %collective-permute-done.3 = bf16[3072,128]{0,1:T(8,128)(2,1)} collective-permute-done((bf16[3072,128]{0,1:T(8,128)(2,1)}, bf16[3072,128]{0,1:T(8,128)(2,1)}, u32[]{:S(2)}, u32[]{:S(2)}) %collective-permute-start.3) | collective-permute-done | bytes 786464 | tf_op jit(solution)/shard_map/ppermute | solution.py:16
  772.5 2.6 collective-permute-start.4
  775.1 9.1 %collective-permute-done.4 = bf16[3072,64]{0,1:T(8,128)(2,1)S(1)} collective-permute-done((bf16[3072,64]{0,1:T(8,128)(2,1)S(1)}, bf16[3072,64]{0,1:T(8,128)(2,1)S(1)}, u32[]{:S(2)}, u32[]{:S(2)}) %collective-permute-start.4) | collective-permute-done | bytes 393248 | tf_op jit(solution)/shard_map/ppermute | solution.py:16
  787.7 14.1 %collective-permute-done.5 = bf16[1536,64]{0,1:T(8,128)(2,1)S(1)} collective-permute-done((bf16[1536,64]{0,1:T(8,128)(2,1)S(1)}, bf16[1536,64]{0,1:T(8,128)(2,1)S(1)}, u32[]{:S(2)}, u32[]{:S(2)}) %collective-permute-start.5) | collective-permute-done | bytes 196640 | tf_op jit(solution)/shard_map/ppermute | solution.py:16
  803.9 7.3 collective-permute-done.6
  813.2 3.8 collective-permute-done.7
  817.1 12.4 %collective-permute-start.8 = (bf16[192,64]{0,1:T(8,128)(2,1)S(1)}, bf16[192,64]{0,1:T(8,128)(2,1)S(1)}, u32[]{:S(2)}, u32[]{:S(2)}) collective-permute-start(bf16[192,64]{0,1:T(8,128)(2,1)S(1)} %select_convert_fusion.5), channel_id=1, source_target_pairs={{0,2},{1,3},{2,0},{3,1},{4,6},{5,7},{6,4},{7,5},{8,10},{9,11},{10,... | collective-permute-start | bytes 73736 | tf_op jit(solution)/shard_map/ppermute | solution.py:16
  829.5 2.3 collective-permute-done.8
  832.0 15.2 %collective-permute-start.9 = (bf16[96,64]{0,1:T(8,128)(2,1)S(1)}, bf16[96,64]{0,1:T(8,128)(2,1)S(1)}, u32[]{:S(2)}, u32[]{:S(2)}) collective-permute-start(bf16[96,64]{0,1:T(8,128)(2,1)S(1)} %select_convert_fusion.6), channel_id=1, source_target_pairs={{0,1},{1,0},{2,3},{3,2},{4,5},{5,4},{6,7},{7,6},{8,9},{9,8},{10,11... | collective-permute-start | bytes 36872 | tf_op jit(solution)/shard_map/ppermute | solution.py:16
  (110 shorter events, 39.3 us)
Async XLA Ops:
  7.2 1.7 copy-start
  7.2 264.0 %all-gather.3.cloned.1.call-start = ((), (), s32[]{:S(2)}) async-start(), calls=%async_computation.2 | async-start | bytes 2162688 | tf_op jit(solution)/shard_map/all_gather | solution.py:45
  8.8 743.5 %reduce-scatter.2.cloned.1.call-start = ((), (), s32[]{:S(2)}) async-start(), calls=%async_computation.1 | async-start | bytes 2162688 | tf_op jit(solution)/shard_map/reduce_scatter | solution.py:131
  309.5 0.9 copy-start.2
  310.4 5.3 collective-permute-start
  315.8 7.9 collective-permute-start.1
  324.6 62.1 %collective-permute-start.2 = (bf16[128,1536]{1,0:T(8,128)(2,1)}, bf16[128,1536]{1,0:T(8,128)(2,1)}, u32[]{:S(2)}, u32[]{:S(2)}) collective-permute-start(bf16[128,1536]{1,0:T(8,128)(2,1)} %maximum_select_fusion.2), channel_id=1, source_target_pairs={{0,512},{32,544},{64,576},{96,608},{128,640},{160,672},{192,704},{... | collective-permute-start | bytes 1179656 | tf_op jit(solution)/shard_map/ppermute | solution.py:16
  755.3 14.5 %collective-permute-start.3 = (bf16[3072,128]{0,1:T(8,128)(2,1)}, bf16[3072,128]{0,1:T(8,128)(2,1)}, u32[]{:S(2)}, u32[]{:S(2)}) collective-permute-start(bf16[3072,128]{0,1:T(8,128)(2,1)} %select_convert_fusion), channel_id=1, source_target_pairs={{0,64},{1,65},{2,66},{3,67},{4,68},{5,69},{6,70},{7,71},{8,72},{9,... | collective-permute-start | bytes 2359304 | tf_op jit(solution)/shard_map/ppermute | solution.py:16
  771.3 1.2 copy-start.1
  772.5 11.8 %collective-permute-start.4 = (bf16[3072,64]{0,1:T(8,128)(2,1)S(1)}, bf16[3072,64]{0,1:T(8,128)(2,1)S(1)}, u32[]{:S(2)}, u32[]{:S(2)}) collective-permute-start(bf16[3072,64]{0,1:T(8,128)(2,1)S(1)} %select_convert_fusion.1), channel_id=1, source_target_pairs={{0,32},{1,33},{2,34},{3,35},{4,36},{5,37},{6,38},{7,39},{8,40},{9,... | collective-permute-start | bytes 1179656 | tf_op jit(solution)/shard_map/ppermute | solution.py:16
  785.8 16.0 %collective-permute-start.5 = (bf16[1536,64]{0,1:T(8,128)(2,1)S(1)}, bf16[1536,64]{0,1:T(8,128)(2,1)S(1)}, u32[]{:S(2)}, u32[]{:S(2)}) collective-permute-start(bf16[1536,64]{0,1:T(8,128)(2,1)S(1)} %select_convert_fusion.2), channel_id=1, source_target_pairs={{0,16},{1,17},{2,18},{3,19},{4,20},{5,21},{6,22},{7,23},{8,24},{9,... | collective-permute-start | bytes 589832 | tf_op jit(solution)/shard_map/ppermute | solution.py:16
  801.9 9.3 %collective-permute-start.6 = (bf16[768,64]{0,1:T(8,128)(2,1)S(1)}, bf16[768,64]{0,1:T(8,128)(2,1)S(1)}, u32[]{:S(2)}, u32[]{:S(2)}) collective-permute-start(bf16[768,64]{0,1:T(8,128)(2,1)S(1)} %select_convert_fusion.3), channel_id=1, source_target_pairs={{0,8},{1,9},{2,10},{3,11},{4,12},{5,13},{6,14},{7,15},{8,0},{9,1},... | collective-permute-start | bytes 294920 | tf_op jit(solution)/shard_map/ppermute | solution.py:16
  811.3 5.7 collective-permute-start.7
  817.1 14.7 %collective-permute-start.8 = (bf16[192,64]{0,1:T(8,128)(2,1)S(1)}, bf16[192,64]{0,1:T(8,128)(2,1)S(1)}, u32[]{:S(2)}, u32[]{:S(2)}) collective-permute-start(bf16[192,64]{0,1:T(8,128)(2,1)S(1)} %select_convert_fusion.5), channel_id=1, source_target_pairs={{0,2},{1,3},{2,0},{3,1},{4,6},{5,7},{6,4},{7,5},{8,10},{9,11},{10,... | collective-permute-start | bytes 73736 | tf_op jit(solution)/shard_map/ppermute | solution.py:16
  832.0 16.1 %collective-permute-start.9 = (bf16[96,64]{0,1:T(8,128)(2,1)S(1)}, bf16[96,64]{0,1:T(8,128)(2,1)S(1)}, u32[]{:S(2)}, u32[]{:S(2)}) collective-permute-start(bf16[96,64]{0,1:T(8,128)(2,1)S(1)} %select_convert_fusion.6), channel_id=1, source_target_pairs={{0,1},{1,0},{2,3},{3,2},{4,5},{5,4},{6,7},{7,6},{8,9},{9,8},{10,11... | collective-permute-start | bytes 36872 | tf_op jit(solution)/shard_map/ppermute | solution.py:16
Sparse Core Ops, SparseCore 0:
  11.2 259.9 all-gather.2
  309.6 442.6 reduce-scatter.1
where the time goes:
time: 858 us; the launch traced here: 856 us
  waiting for transfers between devices  721 us (84%)
  starting transfers between devices  66.5 us (8%)
  local copies, waits for them, and re-layouts  32.9 us (4%)
  other arithmetic  14.6 us (2%)
  between operations  14.4 us (2%)
    reduce_scatter x1, waiting for transfers between devices, shards(): lax.psum_scatter(grads_acc.reshape(seq_length, cache_columns).astype(jnp....  366 us
    all_gather x1, waiting for transfers between devices, shards(): window = lax.all_gather(kv_cache[0], 'tok', axis=0, tiled=True)  259 us
    ppermute x10, waiting for transfers between devices, from_partner(): return lax.ppermute(value, axis, pairs)  96.1 us
    ppermute x10, starting transfers between devices, from_partner(): return lax.ppermute(value, axis, pairs)  66.5 us
    convert_element_type x1, local copies, waits for them, and re-layouts, shards(): grads_acc.reshape(seq_length, cache_columns).astype(jnp.bfloat16)  17.8 us
  transfers between devices with their start and end apart: 12, of which 11 were waited for; matrix products, arithmetic and copies ran while one was open for 1% of the time, Pallas kernels for 0%

commit v1 on v0

v1 whole, which is shorter than its diff:
```python
import functools

import jax
import jax.numpy as jnp
from jax import lax
from jax.experimental import pallas as pl
from jax.experimental.pallas import tpu as pltpu
from jax.sharding import PartitionSpec as P

HD = 128
KVH = 8
NEG_FILL = -1e30
PIECES = 2
LOG2E = 1.4426950408889634
CONTRACT_LAST = (((1,), (1,)), ((), ()))
CONTRACT_FIRST = (((0,), (0,)), ((), ()))


def remote(src, dst, send_sem, recv_sem, tok):
    return pltpu.make_async_remote_copy(
        src_ref=src,
        dst_ref=dst,
        send_sem=send_sem,
        recv_sem=recv_sem,
        device_id={"tok": tok},
        device_id_type=pl.DeviceIdType.MESH,
    )


def attention_kernel(
    n_tok,
    doc_lens,
    queries,
    upstream,
    cache,
    query_grads,
    cache_grads,
    qs,
    us,
    window,
    exps,
    dws,
    tops,
    stats,
    dq_acc,
    terms,
    own_terms,
    sib_out,
    sib_in,
    run_out,
    run_in,
    up_send,
    up_recv,
    side_send,
    side_recv,
    back_side_send,
    back_side_recv,
    down_send,
    down_recv,
):
    layers, rows, columns = queries.shape
    heads = columns // HD
    n_rows = layers * heads * rows
    chips = n_tok // 2
    reach = n_tok // 4
    piece = rows // PIECES
    pair = 2 * rows
    n_pairs = n_rows // pair
    scale = HD ** (-0.5)

    tok = lax.axis_index("tok")
    hs = lax.axis_index("hs")
    chip = tok // 2
    core = tok % 2
    sibling = tok + 1 - 2 * core
    above = lax.rem(tok + 2, n_tok)
    below = lax.rem(tok + n_tok - 2, n_tok)
    not_last = chip < chips - 1
    mine = core * rows
    theirs = (1 - core) * rows

    barrier = pltpu.get_barrier_semaphore()
    for other in (sibling, above, below):
        pl.semaphore_signal(
            barrier, inc=1, device_id={"tok": other}, device_id_type=pl.DeviceIdType.MESH
        )
    pl.semaphore_wait(barrier, 3)

    def span(first, i):
        return pl.ds(pl.multiple_of(first + i * piece, piece), piece)

    def up_copy(d, i, from_cache=False):
        src = cache.at[pl.ds(i * piece, piece)] if from_cache else window.at[d - 1, span(mine, i)]
        return remote(src, window.at[d, span(mine, i)], up_send.at[d, i], up_recv.at[d, i], above)

    def side_copy(d, i, from_cache=False):
        src = cache.at[pl.ds(i * piece, piece)] if from_cache else window.at[d, span(mine, i)]
        return remote(
            src, window.at[d, span(mine, i)], side_send.at[d, i], side_recv.at[d, i], sibling
        )

    def side_arrival(d, i):
        dst = window.at[d, span(theirs, i)]
        return remote(dst, dst, side_send.at[d, i], side_recv.at[d, i], sibling)

    for i in range(PIECES):

        @pl.when(not_last)
        def _():
            up_copy(1, i, True).start()

        side_copy(0, i, True).start()

    window[0, pl.ds(pl.multiple_of(mine, rows), rows)] = cache[...]
    for layer in range(layers):
        for head in range(heads):
            at = (layer * heads + head) * rows
            qs[at : at + rows] = queries[layer, :, head * HD : (head + 1) * HD]
            us[at : at + rows] = upstream[layer, :, head * HD : (head + 1) * HD]

    row_top = stats.at[0:1]
    row_total = stats.at[1:2]
    row_weighted = stats.at[2:3]
    row_top[...] = jnp.full((1, n_rows), NEG_FILL, jnp.float32)
    row_total[...] = jnp.zeros((1, n_rows), jnp.float32)
    row_weighted[...] = jnp.zeros((1, n_rows), jnp.float32)

    seq = hs % doc_lens.shape[0]
    position = tok * rows + lax.rem(lax.broadcasted_iota(jnp.int32, (1, pair), 1), rows)
    start = jnp.zeros((1, pair), jnp.int32)
    end = jnp.int32(0)
    for k in range(doc_lens.shape[1] - 1):
        end = end + doc_lens[seq, k]
        start = jnp.where(position >= end, end, start)

    for i in range(PIECES):
        side_arrival(0, i).wait_recv()

    def stats_part(d, n):
        at = pl.ds(n * pair, pair)
        key_rows = window[d, :, 0:HD]
        value_rows = window[d, :, HD : 2 * HD]
        scores = lax.dot_general(
            key_rows, qs[at], CONTRACT_LAST, preferred_element_type=jnp.float32
        )
        dweights = lax.dot_general(
            value_rows, us[at], CONTRACT_LAST, preferred_element_type=jnp.float32
        )
        key_pos = (chip - d) * pair + lax.broadcasted_iota(jnp.int32, (pair, pair), 0)
        allowed = (key_pos <= position) & (key_pos >= start)
        scores = jnp.where(allowed, scores * (scale * LOG2E), NEG_FILL)
        top_old = row_top[:, at]
        top = jnp.maximum(top_old, jnp.max(scores, axis=0, keepdims=True))
        exp_terms = jnp.exp2(scores - top)
        factor = jnp.exp2(top_old - top)
        row_top[:, at] = top
        row_total[:, at] = row_total[:, at] * factor + jnp.sum(exp_terms, axis=0, keepdims=True)
        row_weighted[:, at] = row_weighted[:, at] * factor + jnp.sum(
            exp_terms * dweights, axis=0, keepdims=True
        )
        exps[d, :, at] = exp_terms
        dws[d, :, at] = dweights
        tops[d, :, at] = top

    @pl.loop(0, reach + 1)
    def _(d):
        more = (d < reach) & (chip > d)
        for n in range(n_pairs):

            @pl.when(chip >= d)
            def _():
                stats_part(d, n)

            if n < PIECES:

                @pl.when(more)
                def _():
                    up_copy(d + 1, n).wait_recv()
                    side_copy(d + 1, n).start()

                @pl.when(more & not_last & (d + 1 < reach))
                def _():
                    up_copy(d + 2, n).start()

        @pl.when(more)
        def _():
            for i in range(PIECES):
                side_arrival(d + 1, i).wait_recv()

    inverse = 1.0 / row_total[...]
    row_delta = stats.at[3:4]
    row_delta[...] = row_weighted[...] * inverse
    row_total[...] = inverse
    dq_acc[...] = jnp.zeros_like(dq_acc)
    run_in[reach] = jnp.zeros((rows, 2 * HD), jnp.bfloat16)

    @pl.when(chip == chips - 1)
    def _():
        for d in range(reach):
            run_in[d] = jnp.zeros((rows, 2 * HD), jnp.bfloat16)

    def grads_part(d, n):
        at = pl.ds(n * pair, pair)
        factor = jnp.exp2(tops[d, :, at] - row_top[:, at]) * row_total[:, at]
        weights = exps[d, :, at] * factor
        dscores = (weights * (dws[d, :, at] - row_delta[:, at])).astype(jnp.bfloat16)
        weights = weights.astype(jnp.bfloat16)
        key_rows = window[d, :, 0:HD]
        key_grads = jnp.dot(dscores, qs[at], preferred_element_type=jnp.float32)
        dvalues = jnp.dot(weights, us[at], preferred_element_type=jnp.float32)
        if n == 0:
            terms[:, 0:HD] = key_grads
            terms[:, HD : 2 * HD] = dvalues
        else:
            terms[:, 0:HD] += key_grads
            terms[:, HD : 2 * HD] += dvalues
        dq_acc[:, at] += lax.dot_general(
            key_rows, dscores, CONTRACT_FIRST, preferred_element_type=jnp.float32
        )

    def back_side_copy(d, i):
        at = pl.ds(i * piece, piece)
        return remote(
            sib_out.at[d, at],
            sib_in.at[d, at],
            back_side_send.at[d, i],
            back_side_recv.at[d, i],
            sibling,
        )

    def down_copy(d, i):
        at = pl.ds(i * piece, piece)
        return remote(
            run_out.at[d, at], run_in.at[d - 1, at], down_send.at[d, i], down_recv.at[d - 1, i], below
        )

    def down_arrival(d, i):
        at = pl.ds(i * piece, piece)
        return remote(
            run_out.at[d, at], run_in.at[d, at], down_send.at[d, i], down_recv.at[d, i], below
        )

    def chain_part(d, i):
        back_side_copy(d, i).wait_recv()

        @pl.when(not_last & (d < reach))
        def _():
            down_arrival(d, i).wait_recv()

        at = pl.ds(i * piece, piece)
        return (
            own_terms[d, at]
            + sib_in[d, at].astype(jnp.float32)
            + run_in[d, at].astype(jnp.float32)
        ).astype(jnp.bfloat16)

    def chain_send(d, i):
        run_out[d, pl.ds(i * piece, piece)] = chain_part(d, i)
        down_copy(d, i).start()

    @pl.loop(0, reach + 1)
    def _(step):
        d = reach - step
        for n in range(n_pairs):

            @pl.when(chip >= d)
            def _():
                grads_part(d, n)

            if n < PIECES:

                @pl.when((step > 0) & (chip >= d + 1))
                def _():
                    chain_send(d + 1, n)

        @pl.when(chip >= d)
        def _():
            sent = terms[pl.ds(pl.multiple_of(theirs, rows), rows)]
            sib_out[d, :, 0:HD] = (sent[:, 0:HD] * scale).astype(jnp.bfloat16)
            sib_out[d, :, HD : 2 * HD] = sent[:, HD : 2 * HD].astype(jnp.bfloat16)
            for i in range(PIECES):
                back_side_copy(d, i).start()
            kept = terms[pl.ds(pl.multiple_of(mine, rows), rows)]
            own_terms[d, :, 0:HD] = kept[:, 0:HD] * scale
            own_terms[d, :, HD : 2 * HD] = kept[:, HD : 2 * HD]

    for layer in range(layers):
        for head in range(heads):
            at = (layer * heads + head) * rows
            block = jnp.transpose(dq_acc[:, at : at + rows]) * scale
            query_grads[layer, :, head * HD : (head + 1) * HD] = block.astype(jnp.bfloat16)
    for i in range(PIECES):
        cache_grads[pl.ds(i * piece, piece)] = chain_part(0, i)

    @pl.loop(0, reach + 1)
    def _(d):
        for i in range(PIECES):

            @pl.when(chip >= d)
            def _():
                side_copy(d, i).wait_send()
                back_side_copy(d, i).wait_send()

            @pl.when((chip >= d) & (d > 0))
            def _():
                down_copy(d, i).wait_send()

            @pl.when(not_last & (chip + 1 >= d) & (d > 0))
            def _():
                up_copy(d, i).wait_send()


def attention(queries, out_grads, cache, doc_lens):
    layers, rows, columns = queries.shape
    n_tok = lax.axis_size("tok")
    slots = n_tok // 4 + 1
    n_rows = layers * columns // HD * rows
    pair = 2 * rows
    vmem = pl.BlockSpec(memory_space=pltpu.VMEM)
    sems = pltpu.SemaphoreType.DMA((slots, PIECES))
    block = (slots, rows, 2 * HD)
    return pl.pallas_call(
        functools.partial(attention_kernel, n_tok),
        out_shape=(
            jax.ShapeDtypeStruct(queries.shape, jnp.bfloat16),
            jax.ShapeDtypeStruct(cache.shape, jnp.bfloat16),
        ),
        in_specs=[pl.BlockSpec(memory_space=pltpu.SMEM), vmem, vmem, vmem],
        out_specs=(vmem, vmem),
        scratch_shapes=[
            pltpu.VMEM((n_rows, HD), jnp.bfloat16),
            pltpu.VMEM((n_rows, HD), jnp.bfloat16),
            pltpu.VMEM((slots, pair, 2 * HD), jnp.bfloat16),
            pltpu.VMEM((slots, pair, n_rows), jnp.float32),
            pltpu.VMEM((slots, pair, n_rows), jnp.float32),
            pltpu.VMEM((slots, 1, n_rows), jnp.float32),
            pltpu.VMEM((8, n_rows), jnp.float32),
            pltpu.VMEM((HD, n_rows), jnp.float32),
            pltpu.VMEM((pair, 2 * HD), jnp.float32),
            pltpu.VMEM(block, jnp.float32),
            pltpu.VMEM(block, jnp.bfloat16),
            pltpu.VMEM(block, jnp.bfloat16),
            pltpu.VMEM(block, jnp.bfloat16),
            pltpu.VMEM(block, jnp.bfloat16),
        ]
        + [sems] * 8,
        compiler_params=pltpu.CompilerParams(
            collective_id=0, has_side_effects=True, vmem_limit_bytes=40 * 2**20
        ),
        name="attention",
    )(doc_lens, queries, out_grads, cache)


def from_partner(value, axis, bit):
    mask = 2**bit
    pairs = [(source, source ^ mask) for source in range(lax.axis_size(axis))]
    return lax.ppermute(value, axis, pairs)


def halve_block(total_sum, upper_bit, which_dim):
    half_width = total_sum.shape[which_dim] // 2
    lower_part = lax.slice_in_dim(total_sum, 0, half_width, axis=which_dim)
    upper_part = lax.slice_in_dim(total_sum, half_width, 2 * half_width, axis=which_dim)
    kept_part = jnp.where(upper_bit == 1, upper_part, lower_part)
    sent_part = jnp.where(upper_bit == 1, lower_part, upper_part)
    return (kept_part, sent_part)


def shards(queries, out_grads, kv_cache, features, doc_lens):
    hs_count = lax.axis_size("hs")
    tok_count = lax.axis_size("tok")
    rank_count = min(KVH, hs_count)
    seq_count = hs_count // rank_count
    hs_place = lax.axis_index("hs")
    query_grads, summed = attention(queries[:, 0], out_grads[:, 0], kv_cache[0], doc_lens)
    full_rows = features[0]
    seq_bits = seq_count.bit_length() - 1
    hs_bits = hs_count.bit_length() - 1
    tok_bits = tok_count.bit_length() - 1
    for bit_number in range(seq_bits, hs_bits):
        partner = from_partner(full_rows, "hs", bit_number)
        upper_bit = hs_place >> bit_number & 1
        full_rows = jnp.where(
            upper_bit == 1,
            jnp.concatenate([partner, full_rows], axis=1),
            jnp.concatenate([full_rows, partner], axis=1),
        )
    partial_grads = jnp.einsum("tf,tc->fc", full_rows, summed, preferred_element_type=jnp.float32)
    joined_place = lax.axis_index(("hs", "tok"))
    halvings = [(tok_bits + bit_number, 1) for bit_number in reversed(range(seq_bits))]
    halvings = halvings + [(bit_number, 0) for bit_number in reversed(range(tok_bits))]
    weight_total = partial_grads
    for bit_number, which_dim in halvings:
        upper_bit = joined_place >> bit_number & 1
        kept_part, sent_part = halve_block(weight_total, upper_bit, which_dim)
        weight_total = kept_part + from_partner(
            sent_part.astype(jnp.bfloat16), ("hs", "tok"), bit_number
        ).astype(sent_part.dtype)
    return (query_grads[:, None], summed[None], weight_total)


def solution(mesh):
    placed = (
        P(None, "hs", "tok", None),
        P(None, "hs", "tok", None),
        P("hs", "tok", None),
        P("hs", "tok", None),
        P(),
    )
    return jax.shard_map(
        shards,
        mesh=mesh,
        in_specs=placed,
        out_specs=(P(None, "hs", "tok", None), P("hs", "tok", None), P("tok", "hs")),
        check_vma=False,
    )
```

time: 858 us -> 276 us (0.32)
  waiting for transfers between devices: 721 us -> 70.8 us
  Pallas kernels: 0 us -> 107 us
  local copies, waits for them, and re-layouts: 32.9 us -> 6.58 us
  starting transfers between devices: 66.5 us -> 81.8 us
  between operations: 14.4 us -> 0.9 us
    reduce_scatter x1 -> x0, waiting for transfers between devices: 366 us -> none  [shards(): lax.psum_scatter(grads_acc.reshape(seq_length, cache_columns).astype(jnp....]
    all_gather x1 -> x0, waiting for transfers between devices: 259 us -> none  [shards(): window = lax.all_gather(kv_cache[0], 'tok', axis=0, tiled=True)]
    pallas_call x0 -> x1, Pallas kernels: none -> 107 us  [attention(): pl.pallas_call(functools.partial(attention_kernel, n_tok), out_shape=(jax...]
    ppermute x10, waiting for transfers between devices: 96.1 us -> 70.8 us  [from_partner(): return lax.ppermute(value, axis, pairs)]
    convert_element_type x1 -> x0, local copies, waits for them, and re-layouts: 17.8 us -> none  [shards(): grads_acc.reshape(seq_length, cache_columns).astype(jnp.bfloat16)]
    ppermute x10, starting transfers between devices: 66.5 us -> 81.8 us  [from_partner(): return lax.ppermute(value, axis, pairs)]
  transfers between devices with their start and end apart: 12 -> 10, of which waited for: 11 -> 9; matrix products, arithmetic and copies ran while one was open for 1% -> 0% of each run, Pallas kernels for 0% -> 39%
where the time goes in v1:
time: 276 us
  Pallas kernels  107 us (39%)
  starting transfers between devices  81.8 us (30%)
  waiting for transfers between devices  70.8 us (26%)
  local copies, waits for them, and re-layouts  6.58 us (2%)
  other arithmetic  6.16 us (2%)
    pallas_call x1, Pallas kernels, attention(): pl.pallas_call(functools.partial(attention_kernel, n_tok), out_shape=(jax...  107 us
    ppermute x10, starting transfers between devices, from_partner(): return lax.ppermute(value, axis, pairs)  81.8 us
    ppermute x10, waiting for transfers between devices, from_partner(): return lax.ppermute(value, axis, pairs)  70.8 us
    unnamed x16, local copies, waits for them, and re-layouts  6.58 us
  transfers between devices with their start and end apart: 10, of which 9 were waited for; matrix products, arithmetic and copies ran while one was open for 0% of the time, Pallas kernels for 39%

profile of v1, /device:TPU:1, one launch (start us, length us, event | category | flops | bytes accessed | tf_op | source)
XLA Modules:
  0.0 275.6 jit_solution(10138966079286620432)
XLA Ops:
  0.6 4.0 %collective-permute-start = (bf16[128,384]{1,0:T(8,128)(2,1)}, bf16[128,384]{1,0:T(8,128)(2,1)S(1)}, u32[]{:S(2)}, u32[]{:S(2)}) collective-permute-start(bf16[128,384]{1,0:T(8,128)(2,1)} %bitcast.14), channel_id=1, source_target_pairs={{0,128},{32,160},{64,192},{96,224},{128,0},{160,32},{192,64},{224,... | collective-permute-start | bytes 294920 | tf_op jit(solution)/shard_map/ppermute | solution.py:357
  4.7 2.2 collective-permute-done
  7.9 5.0 %collective-permute-start.1 = (bf16[128,768]{1,0:T(8,128)(2,1)S(1)}, bf16[128,768]{1,0:T(8,128)(2,1)S(1)}, u32[]{:S(2)}, u32[]{:S(2)}) collective-permute-start(bf16[128,768]{1,0:T(8,128)(2,1)S(1)} %maximum_select_fusion.3), channel_id=1, source_target_pairs={{0,256},{32,288},{64,320},{96,352},{128,384},{160,416},{192,448},{... | collective-permute-start | bytes 589832 | tf_op jit(solution)/shard_map/ppermute | solution.py:357
  12.9 3.0 %collective-permute-done.1 = bf16[128,768]{1,0:T(8,128)(2,1)S(1)} collective-permute-done((bf16[128,768]{1,0:T(8,128)(2,1)S(1)}, bf16[128,768]{1,0:T(8,128)(2,1)S(1)}, u32[]{:S(2)}, u32[]{:S(2)}) %collective-permute-start.1) | collective-permute-done | bytes 196640 | tf_op jit(solution)/shard_map/ppermute | solution.py:357
  16.0 28.7 %collective-permute-start.2 = (bf16[128,1536]{1,0:T(8,128)(2,1)S(1)}, bf16[128,1536]{1,0:T(8,128)(2,1)S(1)}, u32[]{:S(2)}, u32[]{:S(2)}) collective-permute-start(bf16[128,1536]{1,0:T(8,128)(2,1)S(1)} %maximum_select_fusion.2), channel_id=1, source_target_pairs={{0,512},{32,544},{64,576},{96,608},{128,640},{160,672},{192,704},{... | collective-permute-start | bytes 1179656 | tf_op jit(solution)/shard_map/ppermute | solution.py:357
  48.2 107.4 %attention.1 = (bf16[2,128,384]{2,1,0:T(8,128)(2,1)S(1)}, bf16[128,256]{1,0:T(8,128)(2,1)S(1)}) custom-call(s32[4,4]{1,0:T(4,128)S(1)} %copy-done.3, bf16[2,128,384]{2,1,0:T(8,128)(2,1)S(1)} %bitcast.10, bf16[2,128,384]{2,1,0:T(8,128)(2,1)S(1)} %bitcast.11, bf16[128,256]{1,0:T(8,128)(2,1)S(1)} %bitcast.13), custom_call_target="tpu_custom_call" | custom-call | tf_op jit(solution)/shard_map/attention/pallas_call | solution.py:322
  156.3 2.0 fusion
  158.3 1.0 select_convert_fusion
  159.3 4.6 %collective-permute-start.3 = (bf16[3072,128]{0,1:T(8,128)(2,1)}, bf16[3072,128]{0,1:T(8,128)(2,1)}, u32[]{:S(2)}, u32[]{:S(2)}) collective-permute-start(bf16[3072,128]{0,1:T(8,128)(2,1)} %select_convert_fusion), channel_id=1, source_target_pairs={{0,64},{1,65},{2,66},{3,67},{4,68},{5,69},{6,70},{7,71},{8,72},{9,... | collective-permute-start | bytes 2359304 | tf_op jit(solution)/shard_map/ppermute | solution.py:357
  164.0 10.3 %collective-permute-done.3 = bf16[3072,128]{0,1:T(8,128)(2,1)} collective-permute-done((bf16[3072,128]{0,1:T(8,128)(2,1)}, bf16[3072,128]{0,1:T(8,128)(2,1)}, u32[]{:S(2)}, u32[]{:S(2)}) %collective-permute-start.3) | collective-permute-done | bytes 786464 | tf_op jit(solution)/shard_map/ppermute | solution.py:357
  174.2 1.4 convert_add_fusion
  175.6 1.2 copy-done.4
  176.9 3.1 %collective-permute-start.4 = (bf16[3072,64]{0,1:T(8,128)(2,1)S(1)}, bf16[3072,64]{0,1:T(8,128)(2,1)S(1)}, u32[]{:S(2)}, u32[]{:S(2)}) collective-permute-start(bf16[3072,64]{0,1:T(8,128)(2,1)S(1)} %select_convert_fusion.1), channel_id=1, source_target_pairs={{0,32},{1,33},{2,34},{3,35},{4,36},{5,37},{6,38},{7,39},{8,40},{9,... | collective-permute-start | bytes 1179656 | tf_op jit(solution)/shard_map/ppermute | solution.py:357
  180.0 6.5 %collective-permute-done.4 = bf16[3072,64]{0,1:T(8,128)(2,1)S(1)} collective-permute-done((bf16[3072,64]{0,1:T(8,128)(2,1)S(1)}, bf16[3072,64]{0,1:T(8,128)(2,1)S(1)}, u32[]{:S(2)}, u32[]{:S(2)}) %collective-permute-start.4) | collective-permute-done | bytes 393248 | tf_op jit(solution)/shard_map/ppermute | solution.py:357
  186.5 1.5 convert_add_fusion.1
  188.0 24.6 %collective-permute-start.5 = (bf16[1536,64]{0,1:T(8,128)(2,1)S(1)}, bf16[1536,64]{0,1:T(8,128)(2,1)S(1)}, u32[]{:S(2)}, u32[]{:S(2)}) collective-permute-start(bf16[1536,64]{0,1:T(8,128)(2,1)S(1)} %select_convert_fusion.2), channel_id=1, source_target_pairs={{0,16},{1,17},{2,18},{3,19},{4,20},{5,21},{6,22},{7,23},{8,24},{9,... | collective-permute-start | bytes 589832 | tf_op jit(solution)/shard_map/ppermute | solution.py:357
  212.6 34.1 %collective-permute-done.5 = bf16[1536,64]{0,1:T(8,128)(2,1)S(1)} collective-permute-done((bf16[1536,64]{0,1:T(8,128)(2,1)S(1)}, bf16[1536,64]{0,1:T(8,128)(2,1)S(1)}, u32[]{:S(2)}, u32[]{:S(2)}) %collective-permute-start.5) | collective-permute-done | bytes 196640 | tf_op jit(solution)/shard_map/ppermute | solution.py:357
  246.8 1.9 collective-permute-start.6
  248.8 7.3 %collective-permute-done.6 = bf16[768,64]{0,1:T(8,128)(2,1)S(1)} collective-permute-done((bf16[768,64]{0,1:T(8,128)(2,1)S(1)}, bf16[768,64]{0,1:T(8,128)(2,1)S(1)}, u32[]{:S(2)}, u32[]{:S(2)}) %collective-permute-start.6) | collective-permute-done | bytes 98336 | tf_op jit(solution)/shard_map/ppermute | solution.py:357
  256.1 1.9 collective-permute-start.7
  258.1 3.8 %collective-permute-done.7 = bf16[384,64]{0,1:T(8,128)(2,1)S(1)} collective-permute-done((bf16[384,64]{0,1:T(8,128)(2,1)S(1)}, bf16[384,64]{0,1:T(8,128)(2,1)S(1)}, u32[]{:S(2)}, u32[]{:S(2)}) %collective-permute-start.7) | collective-permute-done | bytes 49184 | tf_op jit(solution)/shard_map/ppermute | solution.py:357
  262.0 1.9 collective-permute-start.8
  263.9 2.7 collective-permute-done.8
  266.8 6.0 %collective-permute-start.9 = (bf16[96,64]{0,1:T(8,128)(2,1)S(1)}, bf16[96,64]{0,1:T(8,128)(2,1)S(1)}, u32[]{:S(2)}, u32[]{:S(2)}) collective-permute-start(bf16[96,64]{0,1:T(8,128)(2,1)S(1)} %select_convert_fusion.6), channel_id=1, source_target_pairs={{0,1},{1,0},{2,3},{3,2},{4,5},{5,4},{6,7},{7,6},{8,9},{9,8},{10,11... | collective-permute-start | bytes 36872 | tf_op jit(solution)/shard_map/ppermute | solution.py:357
  (30 shorter events, 8.5 us)
Async XLA Ops:
  0.6 6.2 %collective-permute-start = (bf16[128,384]{1,0:T(8,128)(2,1)}, bf16[128,384]{1,0:T(8,128)(2,1)S(1)}, u32[]{:S(2)}, u32[]{:S(2)}) collective-permute-start(bf16[128,384]{1,0:T(8,128)(2,1)} %bitcast.14), channel_id=1, source_target_pairs={{0,128},{32,160},{64,192},{96,224},{128,0},{160,32},{192,64},{224,... | collective-permute-start | bytes 294920 | tf_op jit(solution)/shard_map/ppermute | solution.py:357
  7.9 8.0 %collective-permute-start.1 = (bf16[128,768]{1,0:T(8,128)(2,1)S(1)}, bf16[128,768]{1,0:T(8,128)(2,1)S(1)}, u32[]{:S(2)}, u32[]{:S(2)}) collective-permute-start(bf16[128,768]{1,0:T(8,128)(2,1)S(1)} %maximum_select_fusion.3), channel_id=1, source_target_pairs={{0,256},{32,288},{64,320},{96,352},{128,384},{160,416},{192,448},{... | collective-permute-start | bytes 589832 | tf_op jit(solution)/shard_map/ppermute | solution.py:357
  16.0 139.5 %copy-start.5 = (bf16[128,1536]{1,0:T(8,128)(2,1)}, bf16[128,1536]{1,0:T(8,128)(2,1)S(1)}, u32[]{:S(2)}) copy-start(bf16[128,1536]{1,0:T(8,128)(2,1)S(1)} %maximum_select_fusion.2) | copy-start | bytes 1179652
  16.0 139.5 %collective-permute-start.2 = (bf16[128,1536]{1,0:T(8,128)(2,1)S(1)}, bf16[128,1536]{1,0:T(8,128)(2,1)S(1)}, u32[]{:S(2)}, u32[]{:S(2)}) collective-permute-start(bf16[128,1536]{1,0:T(8,128)(2,1)S(1)} %maximum_select_fusion.2), channel_id=1, source_target_pairs={{0,512},{32,544},{64,576},{96,608},{128,640},{160,672},{192,704},{... | collective-permute-start | bytes 1179656 | tf_op jit(solution)/shard_map/ppermute | solution.py:357
  44.8 0.9 copy-start
  45.7 0.9 copy-start.1
  46.6 0.8 copy-start.2
  47.5 0.7 copy-start.3
  155.6 0.7 copy-start.6
  159.3 14.9 %collective-permute-start.3 = (bf16[3072,128]{0,1:T(8,128)(2,1)}, bf16[3072,128]{0,1:T(8,128)(2,1)}, u32[]{:S(2)}, u32[]{:S(2)}) collective-permute-start(bf16[3072,128]{0,1:T(8,128)(2,1)} %select_convert_fusion), channel_id=1, source_target_pairs={{0,64},{1,65},{2,66},{3,67},{4,68},{5,69},{6,70},{7,71},{8,72},{9,... | collective-permute-start | bytes 2359304 | tf_op jit(solution)/shard_map/ppermute | solution.py:357
  175.6 1.2 copy-start.4
  176.9 9.6 %collective-permute-start.4 = (bf16[3072,64]{0,1:T(8,128)(2,1)S(1)}, bf16[3072,64]{0,1:T(8,128)(2,1)S(1)}, u32[]{:S(2)}, u32[]{:S(2)}) collective-permute-start(bf16[3072,64]{0,1:T(8,128)(2,1)S(1)} %select_convert_fusion.1), channel_id=1, source_target_pairs={{0,32},{1,33},{2,34},{3,35},{4,36},{5,37},{6,38},{7,39},{8,40},{9,... | collective-permute-start | bytes 1179656 | tf_op jit(solution)/shard_map/ppermute | solution.py:357
  188.0 58.7 %collective-permute-start.5 = (bf16[1536,64]{0,1:T(8,128)(2,1)S(1)}, bf16[1536,64]{0,1:T(8,128)(2,1)S(1)}, u32[]{:S(2)}, u32[]{:S(2)}) collective-permute-start(bf16[1536,64]{0,1:T(8,128)(2,1)S(1)} %select_convert_fusion.2), channel_id=1, source_target_pairs={{0,16},{1,17},{2,18},{3,19},{4,20},{5,21},{6,22},{7,23},{8,24},{9,... | collective-permute-start | bytes 589832 | tf_op jit(solution)/shard_map/ppermute | solution.py:357
  246.8 9.3 %collective-permute-start.6 = (bf16[768,64]{0,1:T(8,128)(2,1)S(1)}, bf16[768,64]{0,1:T(8,128)(2,1)S(1)}, u32[]{:S(2)}, u32[]{:S(2)}) collective-permute-start(bf16[768,64]{0,1:T(8,128)(2,1)S(1)} %select_convert_fusion.3), channel_id=1, source_target_pairs={{0,8},{1,9},{2,10},{3,11},{4,12},{5,13},{6,14},{7,15},{8,0},{9,1},... | collective-permute-start | bytes 294920 | tf_op jit(solution)/shard_map/ppermute | solution.py:357
  256.1 5.7 %collective-permute-start.7 = (bf16[384,64]{0,1:T(8,128)(2,1)S(1)}, bf16[384,64]{0,1:T(8,128)(2,1)S(1)}, u32[]{:S(2)}, u32[]{:S(2)}) collective-permute-start(bf16[384,64]{0,1:T(8,128)(2,1)S(1)} %select_convert_fusion.4), channel_id=1, source_target_pairs={{0,4},{1,5},{2,6},{3,7},{4,0},{5,1},{6,2},{7,3},{8,12},{9,13},{10,... | collective-permute-start | bytes 147464 | tf_op jit(solution)/shard_map/ppermute | solution.py:357
  262.0 4.7 %collective-permute-start.8 = (bf16[192,64]{0,1:T(8,128)(2,1)S(1)}, bf16[192,64]{0,1:T(8,128)(2,1)S(1)}, u32[]{:S(2)}, u32[]{:S(2)}) collective-permute-start(bf16[192,64]{0,1:T(8,128)(2,1)S(1)} %select_convert_fusion.5), channel_id=1, source_target_pairs={{0,2},{1,3},{2,0},{3,1},{4,6},{5,7},{6,4},{7,5},{8,10},{9,11},{10,... | collective-permute-start | bytes 73736 | tf_op jit(solution)/shard_map/ppermute | solution.py:357
  266.8 6.8 %collective-permute-start.9 = (bf16[96,64]{0,1:T(8,128)(2,1)S(1)}, bf16[96,64]{0,1:T(8,128)(2,1)S(1)}, u32[]{:S(2)}, u32[]{:S(2)}) collective-permute-start(bf16[96,64]{0,1:T(8,128)(2,1)S(1)} %select_convert_fusion.6), channel_id=1, source_target_pairs={{0,1},{1,0},{2,3},{3,2},{4,5},{5,4},{6,7},{7,6},{8,9},{9,8},{10,11... | collective-permute-start | bytes 36872 | tf_op jit(solution)/shard_map/ppermute | solution.py:357

commit v2 on v1

v2 whole, which is shorter than its diff:
```python
import functools

import jax
import jax.numpy as jnp
from jax import lax
from jax.experimental import pallas as pl
from jax.experimental.pallas import tpu as pltpu
from jax.sharding import PartitionSpec as P

HD = 128
SEQS = 4
RANKS_Y = 4
GROUP = 4
NEG_FILL = -1e30
PIECES = 2
CROSS_AT = "mid"
LOG2E = 1.4426950408889634
MESH = pl.DeviceIdType.MESH
CONTRACT_LAST = (((1,), (1,)), ((), ()))
CONTRACT_FIRST = (((0,), (0,)), ((), ()))


def remote(src, dst, send_sem, recv_sem, device):
    return pltpu.make_async_remote_copy(
        src_ref=src,
        dst_ref=dst,
        send_sem=send_sem,
        recv_sem=recv_sem,
        device_id=device,
        device_id_type=MESH,
    )


def kernel(
    n_tok,
    doc_lens,
    queries,
    upstream,
    cache,
    features,
    query_grads,
    cache_grads,
    weight_grads,
    qs,
    us,
    window,
    exps,
    dws,
    tops,
    stats,
    dq_acc,
    terms,
    own_terms,
    sib_out,
    sib_in,
    run_out,
    run_in,
    feat_own,
    feat_cross,
    feat_all,
    grads_out,
    grads_in,
    parts,
    core_in,
    near_out,
    near_in,
    far_out,
    far_in,
    last_out,
    last_in,
    up_send,
    up_recv,
    side_send,
    side_recv,
    back_send,
    back_recv,
    down_send,
    down_recv,
    own_send,
    cross_send,
    feat_recv,
    half_send,
    half_recv,
    grads_send,
    grads_recv,
    core_send,
    core_recv,
    near_send,
    near_recv,
    far_send,
    far_recv,
    last_send,
    last_recv,
):
    layers, rows, columns = queries.shape
    heads = columns // HD
    n_rows = layers * heads * rows
    chips = n_tok // 2
    reach = n_tok // 4
    piece = rows // PIECES
    pair = 2 * rows
    n_pairs = n_rows // pair
    scale = HD ** (-0.5)

    tok = lax.axis_index("tok")
    hs = lax.axis_index("hs")
    chip = tok // 2
    core = tok % 2
    sibling = tok + 1 - 2 * core
    mine = core * rows
    theirs = (1 - core) * rows
    x = hs % SEQS
    y = (hs // SEQS) % RANKS_Y
    plane = SEQS * RANKS_Y
    half = hs // plane
    place = hs % plane
    rank = half * RANKS_Y + y
    other_half = (1 - half) * plane + place
    other_rank = (1 - half) * RANKS_Y + y
    beside = hs + 1 - 2 * (x % 2)
    spot = chip % GROUP
    group = chip // GROUP

    def near_tok(k):
        return (group * GROUP + (spot + k) % GROUP) * 2 + core

    def far_tok(k):
        return (((group + k) % GROUP) * GROUP + spot) * 2 + core

    def plane_hs(k):
        return half * plane + (place + k) % plane

    barrier = pltpu.get_barrier_semaphore()
    met = [{"tok": sibling}]
    met += [{"tok": (tok + k) % n_tok} for k in (2, n_tok - 2, 6, n_tok - 6)]
    met += [{"tok": near_tok(k)} for k in range(1, GROUP)]
    met += [{"tok": far_tok(k)} for k in range(1, GROUP)]
    met += [{"hs": plane_hs(k)} for k in range(1, plane)]
    met += [{"hs": other_half}, {"hs": beside, "tok": sibling}]
    for device in met:
        pl.semaphore_signal(barrier, inc=1, device_id=device, device_id_type=MESH)

    for layer in range(layers):
        for head in range(heads):
            at = (layer * heads + head) * rows
            qs[at : at + rows] = queries[layer, :, head * HD : (head + 1) * HD]
            us[at : at + rows] = upstream[layer, :, head * HD : (head + 1) * HD]
    window[0, pl.ds(pl.multiple_of(mine, rows), rows)] = cache[...]

    row_block = features.shape[1] // 4
    for n in range(features.shape[1] // HD):
        turned = jnp.transpose(features[:, n * HD : (n + 1) * HD].astype(jnp.float32)).astype(
            jnp.bfloat16
        )
        first = n * HD
        while first < (n + 1) * HD:
            block = first // row_block
            last = min((block + 1) * row_block, (n + 1) * HD)
            to = (block // 2) * row_block + first - block * row_block
            feat_own[block % 2, to : to + last - first] = turned[
                first - n * HD : last - n * HD
            ]
            first = last

    row_top = stats.at[0:1]
    row_total = stats.at[1:2]
    row_weighted = stats.at[2:3]
    row_top[...] = jnp.full((1, n_rows), NEG_FILL, jnp.float32)
    row_total[...] = jnp.zeros((1, n_rows), jnp.float32)
    row_weighted[...] = jnp.zeros((1, n_rows), jnp.float32)
    dq_acc[...] = jnp.zeros_like(dq_acc)

    seq = x
    position = tok * rows + lax.rem(lax.broadcasted_iota(jnp.int32, (1, pair), 1), rows)
    start = jnp.zeros((1, pair), jnp.int32)
    end = jnp.int32(0)
    for k in range(doc_lens.shape[1] - 1):
        end = end + doc_lens[seq, k]
        start = jnp.where(position >= end, end, start)

    pl.semaphore_wait(barrier, len(met))

    def span(first, i):
        return pl.ds(pl.multiple_of(first + i * piece, piece), piece)

    def up_copy(d, hop, i, from_cache=False):
        src = cache.at[pl.ds(i * piece, piece)] if from_cache else window.at[d - hop, span(mine, i)]
        return remote(
            src,
            window.at[d, span(mine, i)],
            up_send.at[d, i],
            up_recv.at[d, i],
            {"tok": (tok + 2 * hop) % n_tok},
        )

    def side_copy(d, i, from_cache=False):
        src = cache.at[pl.ds(i * piece, piece)] if from_cache else window.at[d, span(mine, i)]
        return remote(
            src,
            window.at[d, span(mine, i)],
            side_send.at[d, i],
            side_recv.at[d, i],
            {"tok": sibling},
        )

    def side_arrival(d, i):
        dst = window.at[d, span(theirs, i)]
        return remote(dst, dst, side_send.at[d, i], side_recv.at[d, i], {"tok": sibling})

    for i in range(PIECES):
        side_copy(0, i, True).start()

        @pl.when(chip + 1 < chips)
        def _():
            up_copy(1, 1, i, True).start()

    for i in range(PIECES):

        @pl.when(chip + 3 < chips)
        def _():
            up_copy(3, 3, i, True).start()

    def own_copy(k):
        to = (place + k) % plane
        return remote(
            feat_own.at[(to % SEQS) % 2],
            feat_all.at[rank, x],
            own_send.at[k],
            feat_recv.at[rank, x],
            {"hs": half * plane + to},
        )

    def cross_copy(k):
        to = (place + k) % plane
        return remote(
            feat_cross.at[(to % SEQS) % 2],
            feat_all.at[other_rank, x],
            cross_send.at[k],
            feat_recv.at[other_rank, x],
            {"hs": half * plane + to},
        )

    def half_copy():
        return remote(feat_own, feat_cross, half_send, half_recv, {"hs": other_half})

    @pl.loop(1, plane)
    def _(k):
        own_copy(k).start()

    feat_all[rank, x] = feat_own[x % 2]

    if CROSS_AT == "start":
        half_copy().start()

    for i in range(PIECES):
        side_arrival(0, i).wait_recv()

    def stats_part(d, n):
        at = pl.ds(n * pair, pair)
        key_rows = window[d, :, 0:HD]
        value_rows = window[d, :, HD : 2 * HD]
        scores = lax.dot_general(
            key_rows, qs[at], CONTRACT_LAST, preferred_element_type=jnp.float32
        )
        dweights = lax.dot_general(
            value_rows, us[at], CONTRACT_LAST, preferred_element_type=jnp.float32
        )
        key_pos = (chip - d) * pair + lax.broadcasted_iota(jnp.int32, (pair, pair), 0)
        allowed = (key_pos <= position) & (key_pos >= start)
        scores = jnp.where(allowed, scores * (scale * LOG2E), NEG_FILL)
        top_old = row_top[:, at]
        top = jnp.maximum(top_old, jnp.max(scores, axis=0, keepdims=True))
        exp_terms = jnp.exp2(scores - top)
        factor = jnp.exp2(top_old - top)
        row_top[:, at] = top
        row_total[:, at] = row_total[:, at] * factor + jnp.sum(exp_terms, axis=0, keepdims=True)
        row_weighted[:, at] = row_weighted[:, at] * factor + jnp.sum(
            exp_terms * dweights, axis=0, keepdims=True
        )
        exps[d, :, at] = exp_terms
        dws[d, :, at] = dweights
        tops[d, :, at] = top

    def stats_block(d):
        @pl.when((chip >= d) & (d <= reach))
        def _():
            for n in range(n_pairs):
                stats_part(d, n)

    def passed_on(d, hop, next_hops):
        for i in range(PIECES):

            @pl.when((chip >= d) & (d <= reach))
            def _():
                up_copy(d, hop, i).wait_recv()
                side_copy(d, i).start()

            for hop_on in next_hops:

                @pl.when((chip >= d) & (d + hop_on <= reach) & (chip + hop_on < chips))
                def _():
                    up_copy(d + hop_on, hop_on, i).start()

    def joined(d):
        for i in range(PIECES):

            @pl.when((chip >= d) & (d <= reach))
            def _():
                side_arrival(d, i).wait_recv()

    @pl.loop(0, reach // 3 + 1)
    def _(turn):
        d = 3 * turn
        stats_block(d)
        passed_on(d + 1, 1, (1,))
        passed_on(d + 3, 3, (3, 1))
        joined(d + 1)
        stats_block(d + 1)
        passed_on(d + 2, 1, ())
        joined(d + 2)
        stats_block(d + 2)
        joined(d + 3)

    if CROSS_AT == "mid":
        half_copy().start()

    inverse = 1.0 / row_total[...]
    row_delta = stats.at[3:4]
    row_delta[...] = row_weighted[...] * inverse
    row_total[...] = inverse

    def grads_part(d, n):
        at = pl.ds(n * pair, pair)
        factor = jnp.exp2(tops[d, :, at] - row_top[:, at]) * row_total[:, at]
        weights = exps[d, :, at] * factor
        dscores = (weights * (dws[d, :, at] - row_delta[:, at])).astype(jnp.bfloat16)
        weights = weights.astype(jnp.bfloat16)
        key_rows = window[d, :, 0:HD]
        key_grads = jnp.dot(dscores, qs[at], preferred_element_type=jnp.float32)
        dvalues = jnp.dot(weights, us[at], preferred_element_type=jnp.float32)
        if n == 0:
            terms[:, 0:HD] = key_grads
            terms[:, HD : 2 * HD] = dvalues
        else:
            terms[:, 0:HD] += key_grads
            terms[:, HD : 2 * HD] += dvalues
        dq_acc[:, at] += lax.dot_general(
            key_rows, dscores, CONTRACT_FIRST, preferred_element_type=jnp.float32
        )

    def rows_of(i):
        return pl.ds(i * piece, piece)

    def back_copy(d, i):
        return remote(
            sib_out.at[d, rows_of(i)],
            sib_in.at[d, rows_of(i)],
            back_send.at[d, i],
            back_recv.at[d, i],
            {"tok": sibling},
        )

    def down_copy(d, hop, i):
        return remote(
            run_out.at[d, rows_of(i)],
            run_in.at[d, rows_of(i)],
            down_send.at[d, i],
            down_recv.at[d, i],
            {"tok": (tok + n_tok - 2 * hop) % n_tok},
        )

    def grads_block(d):
        @pl.when((chip >= d) & (d <= reach))
        def _():
            for n in range(n_pairs):
                grads_part(d, n)
            sent = terms[pl.ds(pl.multiple_of(theirs, rows), rows)]
            sib_out[d, :, 0:HD] = (sent[:, 0:HD] * scale).astype(jnp.bfloat16)
            sib_out[d, :, HD : 2 * HD] = sent[:, HD : 2 * HD].astype(jnp.bfloat16)
            for i in range(PIECES):
                back_copy(d, i).start()
            kept = terms[pl.ds(pl.multiple_of(mine, rows), rows)]
            own_terms[d, :, 0:HD] = kept[:, 0:HD] * scale
            own_terms[d, :, HD : 2 * HD] = kept[:, HD : 2 * HD]

    def summed(d, i, children):
        back_copy(d, i).wait_recv()
        own_terms[d, rows_of(i)] += sib_in[d, rows_of(i)].astype(jnp.float32)
        for child in children:

            @pl.when((d + child <= reach) & (chip + child < chips))
            def _():
                down_copy(d + child, child, i).wait_recv()
                own_terms[d, rows_of(i)] += run_in[d + child, rows_of(i)].astype(jnp.float32)

    def sent_down(d, hop, children):
        for i in range(PIECES):

            @pl.when((chip >= d) & (d <= reach))
            def _():
                summed(d, i, children)
                run_out[d, rows_of(i)] = own_terms[d, rows_of(i)].astype(jnp.bfloat16)
                down_copy(d, hop, i).start()

    @pl.loop(0, reach // 3 + 1)
    def _(turn):
        d = 3 * (reach // 3 - turn)
        grads_block(d + 2)
        grads_block(d + 1)
        sent_down(d + 4, 1, (1,))
        sent_down(d + 2, 1, ())
        sent_down(d + 6, 3, (1, 3))
        grads_block(d)

    for layer in range(layers):
        for head in range(heads):
            at = (layer * heads + head) * rows
            block = jnp.transpose(dq_acc[:, at : at + rows]) * scale
            query_grads[layer, :, head * HD : (head + 1) * HD] = block.astype(jnp.bfloat16)
    sent_down(1, 1, (1,))
    sent_down(3, 3, (1, 3))
    for i in range(PIECES):
        summed(0, i, (1, 3))

    for q in range(2):
        cut = own_terms[0, :, q * HD : (q + 1) * HD].astype(jnp.bfloat16)
        cache_grads[:, q * HD : (q + 1) * HD] = cut
        grads_out[q] = cut

    def grads_copy(k):
        to = (x + k) % SEQS
        return remote(
            grads_out.at[to // 2],
            grads_in.at[pl.ds(pl.multiple_of(x * rows, rows), rows)],
            grads_send.at[k],
            grads_recv.at[x],
            {"hs": hs - x + to},
        )

    def grads_arrival(k):
        came = (x + SEQS - k) % SEQS
        return remote(
            grads_out.at[0],
            grads_in.at[pl.ds(pl.multiple_of(came * rows, rows), rows)],
            grads_send.at[k],
            grads_recv.at[came],
            {"hs": hs},
        )

    for k in range(1, SEQS):
        grads_copy(k).start()
    grads_in[pl.ds(pl.multiple_of(x * rows, rows), rows)] = grads_out[x // 2]

    half_copy().wait_recv()

    @pl.loop(1, plane)
    def _(k):
        cross_copy(k).start()

    feat_all[other_rank, x] = feat_cross[x % 2]

    def feat_arrival(from_rank, k):
        came = (place + k) % plane
        came_rank = (from_rank // RANKS_Y) * RANKS_Y + came // SEQS
        dst = feat_all.at[came_rank, came % SEQS]
        return remote(
            dst, dst, own_send.at[k], feat_recv.at[came_rank, came % SEQS], {"hs": hs}
        )

    @pl.loop(1, plane)
    def _(k):
        feat_arrival(rank, k).wait_recv()

    for k in range(1, SEQS):
        grads_arrival(k).wait_recv()

    cut_rows = row_block // 2

    def product(r):
        block = jnp.zeros((2 * row_block, HD), jnp.float32)
        for s in range(SEQS):
            block += jnp.dot(
                feat_all[r, s],
                grads_in[s * rows : (s + 1) * rows],
                preferred_element_type=jnp.float32,
            )
        for j in range(2):
            u = 2 * r + j
            for c in range(2):
                first = j * row_block + c * cut_rows
                parts[c, u % GROUP, u // GROUP] = block[first : first + cut_rows]

    @pl.loop(0, RANKS_Y)
    def _(k):
        product(half * RANKS_Y + k)

    @pl.loop(1, plane)
    def _(k):
        feat_arrival(other_rank, k).wait_recv()

    @pl.loop(0, RANKS_Y)
    def _(k):
        product((1 - half) * RANKS_Y + k)

    def core_copy(v):
        return remote(
            near_out.at[1, v], core_in.at[v], core_send.at[v], core_recv.at[v], {"tok": sibling}
        )

    for k in (1, 2, 3, 0):
        v = (spot + k) % GROUP
        near_out[1, v] = parts[1 - core, v].astype(jnp.bfloat16)
        core_copy(v).start()

    def near_copy(k):
        v = (spot + k) % GROUP
        return remote(
            near_out.at[0, v],
            near_in.at[GROUP - k],
            near_send.at[k],
            near_recv.at[GROUP - k],
            {"tok": near_tok(k)},
        )

    for k in (1, 2, 3, 0):
        v = (spot + k) % GROUP
        core_copy(v).wait_recv()
        total = parts[core, v] + core_in[v].astype(jnp.float32)
        if k == 0:
            parts[core, v] = total
        else:
            near_out[0, v] = total.astype(jnp.bfloat16)
            near_copy(k).start()

    def near_arrival(k):
        return remote(
            near_out.at[0, spot], near_in.at[k], near_send.at[k], near_recv.at[k], {"tok": tok}
        )

    for k in range(1, GROUP):
        near_arrival(k).wait_recv()
        parts[core, spot] += near_in[k].astype(jnp.float32)

    def far_copy(k):
        return remote(
            far_out.at[k],
            far_in.at[GROUP - k],
            far_send.at[k],
            far_recv.at[GROUP - k],
            {"tok": far_tok(k)},
        )

    for k in range(1, GROUP):
        far_out[k] = parts[core, spot, (group + k) % GROUP].astype(jnp.bfloat16)
        far_copy(k).start()

    def far_arrival(k):
        return remote(far_out.at[k], far_in.at[k], far_send.at[k], far_recv.at[k], {"tok": tok})

    total = parts[core, spot, group]
    for k in range(1, GROUP):
        far_arrival(k).wait_recv()
        total = total + far_in[k].astype(jnp.float32)
    last_out[...] = total

    parity = x % 2
    owner = tok - core + parity
    same_core = core == parity

    def last_copy(to_hs, k):
        return remote(
            last_out, last_in.at[core], last_send.at[k], last_recv.at[core],
            {"hs": to_hs, "tok": owner},
        )

    last_copy(beside, 1).start()

    @pl.when(same_core)
    def _():
        last_in[core] = total

    @pl.when(jnp.logical_not(same_core))
    def _():
        last_copy(hs, 0).start()

    def last_arrival(c):
        return remote(
            last_out, last_in.at[c], last_send.at[0], last_recv.at[c], {"hs": hs, "tok": tok}
        )

    for c in range(2):

        @pl.when(jnp.logical_not(same_core & (core == c)))
        def _():
            last_arrival(c).wait_recv()

        block = last_in[c]
        width = weight_grads.shape[1]
        weight_grads[c * cut_rows : (c + 1) * cut_rows] = jnp.where(
            parity == 0, block[:, 0:width], block[:, width : 2 * width]
        )

    last_copy(beside, 1).wait_send()

    @pl.when(jnp.logical_not(same_core))
    def _():
        last_copy(hs, 0).wait_send()

    for k in range(1, GROUP):
        far_copy(k).wait_send()
        near_copy(k).wait_send()
        grads_copy(k).wait_send()
    for v in range(GROUP):
        core_copy(v).wait_send()
    half_copy().wait_send()

    @pl.loop(1, plane)
    def _(k):
        own_copy(k).wait_send()
        cross_copy(k).wait_send()

    @pl.loop(0, reach + 1)
    def _(d):
        for i in range(PIECES):

            @pl.when(chip >= d)
            def _():
                side_copy(d, i).wait_send()
                back_copy(d, i).wait_send()

            for last, hop in ((d % 3 != 0, 1), ((d % 3 == 0) & (d > 0), 3)):

                @pl.when((chip >= d) & last)
                def _():
                    down_copy(d, hop, i).wait_send()

                @pl.when((chip + hop >= d) & (chip + hop < chips) & last)
                def _():
                    up_copy(d, hop, i).wait_send()


def shards(queries, out_grads, kv_cache, features, doc_lens):
    layers, _, rows, columns = queries.shape
    feats = features.shape[2]
    n_tok = lax.axis_size("tok")
    slots = n_tok // 4 + 1
    n_rows = layers * columns // HD * rows
    pair = 2 * rows
    ranks = 2 * RANKS_Y
    cut = feats // 8
    vmem = pl.BlockSpec(memory_space=pltpu.VMEM)
    dma = pltpu.SemaphoreType.DMA
    sems = dma((slots, PIECES))
    block = (slots, rows, 2 * HD)
    bf16, f32 = jnp.bfloat16, jnp.float32
    query_grads, cache_grads, weight_grads = pl.pallas_call(
        functools.partial(kernel, n_tok),
        out_shape=(
            jax.ShapeDtypeStruct((layers, rows, columns), bf16),
            jax.ShapeDtypeStruct((rows, 2 * HD), bf16),
            jax.ShapeDtypeStruct((feats // 4, 2 * HD // SEQS), f32),
        ),
        in_specs=[pl.BlockSpec(memory_space=pltpu.SMEM), vmem, vmem, vmem, vmem],
        out_specs=(vmem, vmem, vmem),
        scratch_shapes=[
            pltpu.VMEM((n_rows, HD), bf16),
            pltpu.VMEM((n_rows, HD), bf16),
            pltpu.VMEM((slots, pair, 2 * HD), bf16),
            pltpu.VMEM((slots, pair, n_rows), f32),
            pltpu.VMEM((slots, pair, n_rows), f32),
            pltpu.VMEM((slots, 1, n_rows), f32),
            pltpu.VMEM((8, n_rows), f32),
            pltpu.VMEM((HD, n_rows), f32),
            pltpu.VMEM((pair, 2 * HD), f32),
            pltpu.VMEM(block, f32),
            pltpu.VMEM(block, bf16),
            pltpu.VMEM(block, bf16),
            pltpu.VMEM(block, bf16),
            pltpu.VMEM(block, bf16),
            pltpu.VMEM((2, feats // 2, rows), bf16),
            pltpu.VMEM((2, feats // 2, rows), bf16),
            pltpu.VMEM((ranks, SEQS, feats // 2, rows), bf16),
            pltpu.VMEM((2, rows, HD), bf16),
            pltpu.VMEM((SEQS * rows, HD), bf16),
            pltpu.VMEM((2, GROUP, GROUP, cut, HD), f32),
            pltpu.VMEM((GROUP, GROUP, cut, HD), bf16),
            pltpu.VMEM((2, GROUP, GROUP, cut, HD), bf16),
            pltpu.VMEM((GROUP, GROUP, cut, HD), bf16),
            pltpu.VMEM((GROUP, cut, HD), bf16),
            pltpu.VMEM((GROUP, cut, HD), bf16),
            pltpu.VMEM((cut, HD), f32),
            pltpu.VMEM((2, cut, HD), f32),
        ]
        + [sems] * 8
        + [dma((16,)), dma((16,)), dma((ranks, SEQS)), dma, dma]
        + [dma((4,))] * 8
        + [dma((2,))] * 2,
        compiler_params=pltpu.CompilerParams(
            collective_id=0, has_side_effects=True, vmem_limit_bytes=48 * 2**20
        ),
        name="backward",
    )(doc_lens, queries[:, 0], out_grads[:, 0], kv_cache[0], features[0])
    return (query_grads[:, None], cache_grads[None], weight_grads)


def solution(mesh):
    placed = (
        P(None, "hs", "tok", None),
        P(None, "hs", "tok", None),
        P("hs", "tok", None),
        P("hs", "tok", None),
        P(),
    )
    return jax.shard_map(
        shards,
        mesh=mesh,
        in_specs=placed,
        out_specs=(P(None, "hs", "tok", None), P("hs", "tok", None), P("tok", "hs")),
        check_vma=False,
    )
```

time: 276 us -> 128 us (0.46)
  starting transfers between devices: 81.8 us -> 0 us
  waiting for transfers between devices: 70.8 us -> 0 us
  Pallas kernels: 107 us -> 120 us
  other arithmetic: 6.16 us -> 0 us
    ppermute x10 -> x0, starting transfers between devices: 81.8 us -> none  [from_partner(): return lax.ppermute(value, axis, pairs)]
    ppermute x10 -> x0, waiting for transfers between devices: 70.8 us -> none  [from_partner(): return lax.ppermute(value, axis, pairs)]
    pallas_call x1, Pallas kernels: 107 us -> 120 us  [shards(): pl.pallas_call(functools.partial(kernel, n_tok), out_shape=(jax.ShapeDtyp...]
    add x7 -> x0, other arithmetic: 3.7 us -> none  [shards(): kept_part + from_partner(sent_part.astype(jnp.bfloat16), ('hs', 'tok'), b...]
    unnamed x16 -> x13, local copies, waits for them, and re-layouts: 6.58 us -> 6.26 us
  transfers between devices with their start and end apart: 10 -> 0, of which waited for: 9 -> 0; matrix products, arithmetic and copies ran while one was open for 0% -> 0% of each run, Pallas kernels for 39% -> 0%
where the time goes in v2:
time: 128 us; the launch traced here: 126 us
  Pallas kernels  120 us (94%)
  local copies, waits for them, and re-layouts  6.26 us (5%)
    pallas_call x1, Pallas kernels, shards(): pl.pallas_call(functools.partial(kernel, n_tok), out_shape=(jax.ShapeDtyp...  120 us
    unnamed x13, local copies, waits for them, and re-layouts  6.26 us

profile of v2, /device:TPU:1, one launch (start us, length us, event | category | flops | bytes accessed | tf_op | source)
XLA Modules:
  0.0 126.5 jit_solution(2172031480111225748)
XLA Ops:
  0.6 0.0 copy-start.4
  0.6 0.7 copy-done.4
  1.3 0.0 copy-start
  1.3 0.9 copy-done
  2.2 0.0 copy-start.1
  2.2 0.9 copy-done.1
  3.2 0.0 copy-start.2
  3.2 0.9 copy-done.2
  4.1 0.0 copy-start.3
  4.1 0.8 copy-done.3
  4.9 119.6 %backward.1 = (bf16[2,128,384]{2,1,0:T(8,128)(2,1)S(1)}, bf16[128,256]{1,0:T(8,128)(2,1)S(1)}, f32[96,64]{1,0:T(8,128)S(1)}) custom-call(s32[4,4]{1,0:T(4,128)S(1)} %copy-done.4, bf16[2,128,384]{2,1,0:T(8,128)(2,1)S(1)} %bitcast.8, bf16[2,128,384]{2,1,0:T(8,128)(2,1)S(1)} %bitcast.9, bf16[128,256]{1,0:T(8,128)(2,1)S(1)} %bitcast.12, ...), custom_call_target="tpu_custom_call" | custom-call | tf_op jit(solution)/shard_map/backward/pallas_call | solution.py:656
  124.5 0.7 copy.9
  125.2 0.7 copy.12
  125.9 0.6 copy.13
Async XLA Ops:
  0.6 0.7 copy-start.4
  1.3 0.9 copy-start
  2.2 0.9 copy-start.1
  3.2 0.9 copy-start.2
  4.1 0.8 copy-start.3

commit v3 on v2

--- a/solution.py
+++ b/solution.py
@@ -13,7 +13,6 @@
 GROUP = 4
 NEG_FILL = -1e30
 PIECES = 2
-CROSS_AT = "mid"
 LOG2E = 1.4426950408889634
 MESH = pl.DeviceIdType.MESH
 CONTRACT_LAST = (((1,), (1,)), ((), ()))
@@ -55,7 +54,9 @@
     sib_in,
     run_out,
     run_in,
+    feat_in,
     feat_own,
+    feat_relay,
     feat_cross,
     feat_all,
     grads_out,
@@ -79,8 +80,9 @@
     own_send,
     cross_send,
     feat_recv,
-    half_send,
-    half_recv,
+    leg_send,
+    leg_recv,
+    load_sems,
     grads_send,
     grads_recv,
     core_send,
@@ -115,7 +117,14 @@
     half = hs // plane
     place = hs % plane
     rank = half * RANKS_Y + y
+    upper = chip // (chips // 2)
+    opposite = (tok + n_tok // 2) % n_tok
+    kept_half = half * plane + place
     other_half = (1 - half) * plane + place
+    leg_hs = (
+        kept_half * upper + other_half * (1 - upper),
+        kept_half * (1 - upper) + other_half * upper,
+    )
     other_rank = (1 - half) * RANKS_Y + y
     beside = hs + 1 - 2 * (x % 2)
     spot = chip % GROUP
@@ -132,24 +141,57 @@
 
     barrier = pltpu.get_barrier_semaphore()
     met = [{"tok": sibling}]
-    met += [{"tok": (tok + k) % n_tok} for k in (2, n_tok - 2, 6, n_tok - 6)]
     met += [{"tok": near_tok(k)} for k in range(1, GROUP)]
     met += [{"tok": far_tok(k)} for k in range(1, GROUP)]
     met += [{"hs": plane_hs(k)} for k in range(1, plane)]
-    met += [{"hs": other_half}, {"hs": beside, "tok": sibling}]
+    met += [{"hs": leg_hs[0], "tok": opposite}, {"hs": leg_hs[1], "tok": opposite}]
+    met += [{"hs": beside, "tok": sibling}]
+    expected = len(met)
+    for k in (1, 3):
+
+        @pl.when(chip + k < chips)
+        def _():
+            pl.semaphore_signal(
+                barrier, inc=1, device_id={"tok": (tok + 2 * k) % n_tok}, device_id_type=MESH
+            )
+
+        @pl.when(chip >= k)
+        def _():
+            pl.semaphore_signal(
+                barrier,
+                inc=1,
+                device_id={"tok": (tok + n_tok - 2 * k) % n_tok},
+                device_id_type=MESH,
+            )
+
+        expected = expected + (2 * chips - 1 - k - chip) // chips + (chip + chips - k) // chips
     for device in met:
         pl.semaphore_signal(barrier, inc=1, device_id=device, device_id_type=MESH)
 
+    loads = [
+        pltpu.make_async_copy(
+            cache, window.at[0, pl.ds(pl.multiple_of(mine, rows), rows)], load_sems.at[0]
+        ),
+        pltpu.make_async_copy(features, feat_in, load_sems.at[1]),
+    ]
     for layer in range(layers):
         for head in range(heads):
             at = (layer * heads + head) * rows
-            qs[at : at + rows] = queries[layer, :, head * HD : (head + 1) * HD]
-            us[at : at + rows] = upstream[layer, :, head * HD : (head + 1) * HD]
-    window[0, pl.ds(pl.multiple_of(mine, rows), rows)] = cache[...]
-
-    row_block = features.shape[1] // 4
-    for n in range(features.shape[1] // HD):
-        turned = jnp.transpose(features[:, n * HD : (n + 1) * HD].astype(jnp.float32)).astype(
+            for source, target in ((queries, qs), (upstream, us)):
+                loads.append(
+                    pltpu.make_async_copy(
+                        source.at[layer, :, head * HD : (head + 1) * HD],
+                        target.at[at : at + rows],
+                        load_sems.at[len(loads)],
+                    )
+                )
+    for load in loads:
+        load.start()
+    loads[1].wait()
+
+    row_block = feat_in.shape[1] // 4
+    for n in range(feat_in.shape[1] // HD):
+        turned = jnp.transpose(feat_in[:, n * HD : (n + 1) * HD].astype(jnp.float32)).astype(
             jnp.bfloat16
         )
         first = n * HD
@@ -178,25 +220,24 @@
         end = end + doc_lens[seq, k]
         start = jnp.where(position >= end, end, start)
 
-    pl.semaphore_wait(barrier, len(met))
+    loads[0].wait()
+    pl.semaphore_wait(barrier, expected)
 
     def span(first, i):
         return pl.ds(pl.multiple_of(first + i * piece, piece), piece)
 
-    def up_copy(d, hop, i, from_cache=False):
-        src = cache.at[pl.ds(i * piece, piece)] if from_cache else window.at[d - hop, span(mine, i)]
-        return remote(
-            src,
+    def up_copy(d, hop, i):
+        return remote(
+            window.at[d - hop, span(mine, i)],
             window.at[d, span(mine, i)],
             up_send.at[d, i],
             up_recv.at[d, i],
             {"tok": (tok + 2 * hop) % n_tok},
         )
 
-    def side_copy(d, i, from_cache=False):
-        src = cache.at[pl.ds(i * piece, piece)] if from_cache else window.at[d, span(mine, i)]
-        return remote(
-            src,
+    def side_copy(d, i):
+        return remote(
+            window.at[d, span(mine, i)],
             window.at[d, span(mine, i)],
             side_send.at[d, i],
             side_recv.at[d, i],
@@ -208,17 +249,17 @@
         return remote(dst, dst, side_send.at[d, i], side_recv.at[d, i], {"tok": sibling})
 
     for i in range(PIECES):
-        side_copy(0, i, True).start()
+        side_copy(0, i).start()
 
         @pl.when(chip + 1 < chips)
         def _():
-            up_copy(1, 1, i, True).start()
+            up_copy(1, 1, i).start()
 
     for i in range(PIECES):
 
         @pl.when(chip + 3 < chips)
         def _():
-            up_copy(3, 3, i, True).start()
+            up_copy(3, 3, i).start()
 
     def own_copy(k):
         to = (place + k) % plane
@@ -240,8 +281,26 @@
             {"hs": half * plane + to},
         )
 
-    def half_copy():
-        return remote(feat_own, feat_cross, half_send, half_recv, {"hs": other_half})
+    def leg_copy(leg, p):
+        source, target = ((feat_own, feat_relay), (feat_relay, feat_cross))[leg]
+        return remote(
+            source.at[p],
+            target.at[p],
+            leg_send.at[leg, p],
+            leg_recv.at[leg, p],
+            {"hs": leg_hs[p], "tok": opposite},
+        )
+
+    def spread(p):
+        first = (p + place) % 2
+
+        @pl.loop(0, plane // 2)
+        def _(m):
+            @pl.when(first + 2 * m > 0)
+            def _():
+                cross_copy(first + 2 * m).start()
+
+    leg_copy(0, 0).start()
 
     @pl.loop(1, plane)
     def _(k):
@@ -249,8 +308,8 @@
 
     feat_all[rank, x] = feat_own[x % 2]
 
-    if CROSS_AT == "start":
-        half_copy().start()
+    for load in loads[2:]:
+        load.wait()
 
     for i in range(PIECES):
         side_arrival(0, i).wait_recv()
@@ -311,6 +370,16 @@
     @pl.loop(0, reach // 3 + 1)
     def _(turn):
         d = 3 * turn
+
+        @pl.when(turn == 1)
+        def _():
+            leg_copy(0, 1).start()
+
+        @pl.when(turn == 2)
+        def _():
+            leg_copy(0, 0).wait_recv()
+            leg_copy(1, 0).start()
+
         stats_block(d)
         passed_on(d + 1, 1, (1,))
         passed_on(d + 3, 3, (3, 1))
@@ -321,8 +390,8 @@
         stats_block(d + 2)
         joined(d + 3)
 
-    if CROSS_AT == "mid":
-        half_copy().start()
+    leg_copy(0, 1).wait_recv()
+    leg_copy(1, 1).start()
 
     inverse = 1.0 / row_total[...]
     row_delta = stats.at[3:4]
@@ -412,6 +481,11 @@
         sent_down(d + 6, 3, (1, 3))
         grads_block(d)
 
+        @pl.when(turn == 1)
+        def _():
+            leg_copy(1, 0).wait_recv()
+            spread(0)
+
     for layer in range(layers):
         for head in range(heads):
             at = (layer * heads + head) * rows
@@ -419,6 +493,9 @@
             query_grads[layer, :, head * HD : (head + 1) * HD] = block.astype(jnp.bfloat16)
     sent_down(1, 1, (1,))
     sent_down(3, 3, (1, 3))
+    leg_copy(1, 1).wait_recv()
+    spread(1)
+    feat_all[other_rank, x] = feat_cross[x % 2]
     for i in range(PIECES):
         summed(0, i, (1, 3))
 
@@ -450,14 +527,6 @@
     for k in range(1, SEQS):
         grads_copy(k).start()
     grads_in[pl.ds(pl.multiple_of(x * rows, rows), rows)] = grads_out[x // 2]
-
-    half_copy().wait_recv()
-
-    @pl.loop(1, plane)
-    def _(k):
-        cross_copy(k).start()
-
-    feat_all[other_rank, x] = feat_cross[x % 2]
 
     def feat_arrival(from_rank, k):
         came = (place + k) % plane
@@ -612,7 +681,9 @@
         grads_copy(k).wait_send()
     for v in range(GROUP):
         core_copy(v).wait_send()
-    half_copy().wait_send()
+    for leg in range(2):
+        for p in range(2):
+            leg_copy(leg, p).wait_send()
 
     @pl.loop(1, plane)
     def _(k):
@@ -660,7 +731,7 @@
             jax.ShapeDtypeStruct((rows, 2 * HD), bf16),
             jax.ShapeDtypeStruct((feats // 4, 2 * HD // SEQS), f32),
         ),
-        in_specs=[pl.BlockSpec(memory_space=pltpu.SMEM), vmem, vmem, vmem, vmem],
+        in_specs=[pl.BlockSpec(memory_space=pltpu.SMEM)] + [pl.BlockSpec(memory_space=pl.ANY)] * 4,
         out_specs=(vmem, vmem, vmem),
         scratch_shapes=[
             pltpu.VMEM((n_rows, HD), bf16),
@@ -677,6 +748,8 @@
             pltpu.VMEM(block, bf16),
             pltpu.VMEM(block, bf16),
             pltpu.VMEM(block, bf16),
+            pltpu.VMEM((rows, feats), bf16),
+            pltpu.VMEM((2, feats // 2, rows), bf16),
             pltpu.VMEM((2, feats // 2, rows), bf16),
             pltpu.VMEM((2, feats // 2, rows), bf16),
             pltpu.VMEM((ranks, SEQS, feats // 2, rows), bf16),
@@ -692,11 +765,12 @@
             pltpu.VMEM((2, cut, HD), f32),
         ]
         + [sems] * 8
-        + [dma((16,)), dma((16,)), dma((ranks, SEQS)), dma, dma]
+        + [dma((16,)), dma((16,)), dma((ranks, SEQS)), dma((2, 2)), dma((2, 2))]
+        + [dma((2 + 2 * layers * columns // HD,))]
         + [dma((4,))] * 8
         + [dma((2,))] * 2,
         compiler_params=pltpu.CompilerParams(
-            collective_id=0, has_side_effects=True, vmem_limit_bytes=48 * 2**20
+            collective_id=0, has_side_effects=True, vmem_limit_bytes=60 * 2**20
         ),
         name="backward",
     )(doc_lens, queries[:, 0], out_grads[:, 0], kv_cache[0], features[0])

time: 128 us -> 118 us (0.922)
  Pallas kernels: 120 us -> 113 us
  local copies, waits for them, and re-layouts: 6.26 us -> 3.78 us
    pallas_call x1, Pallas kernels: 120 us -> 113 us  [shards(): pl.pallas_call(functools.partial(kernel, n_tok), out_shape=(jax.ShapeDtyp...]
    unnamed x13 -> x5, local copies, waits for them, and re-layouts: 6.26 us -> 3.78 us
where the time goes in v3:
time: 118 us; the launch traced here: 117 us
  Pallas kernels  113 us (96%)
  local copies, waits for them, and re-layouts  3.78 us (3%)
    pallas_call x1, Pallas kernels, shards(): pl.pallas_call(functools.partial(kernel, n_tok), out_shape=(jax.ShapeDtyp...  113 us
    unnamed x5, local copies, waits for them, and re-layouts  3.78 us

profile of v3, /device:TPU:1, one launch (start us, length us, event | category | flops | bytes accessed | tf_op | source)
XLA Modules:
  0.0 117.3 jit_solution(867942341948750668)
XLA Ops:
  0.6 112.9 %backward.1 = (bf16[2,128,384]{2,1,0:T(8,128)(2,1)}, bf16[128,256]{1,0:T(8,128)(2,1)}, f32[96,64]{1,0:T(8,128)}) custom-call(s32[4,4]{1,0:T(4,128)} %doc_lens.1, bf16[2,128,384]{2,1,0:T(8,128)(2,1)} %bitcast.8, bf16[2,128,384]{2,1,0:T(8,128)(2,1)} %bitcast.9, bf16[128,256]{1,0:T(8,128)(2,1)} %bitcast.12, bf16[128,384]{1,0:T(8,128)(2,1)} %bitcast.11), custom_call_target="tpu_custom_call" | custom-call | tf_op jit(solution)/shard_map/backward/pallas_call | solution.py:727
  113.5 1.5 %copy.9 = f32[96,64]{0,1:T(8,128)} copy(f32[96,64]{1,0:T(8,128)} %get-tuple-element.11) | data formatting | bytes 49152
  115.0 0.0 copy-start
  115.0 1.7 %copy.12 = bf16[2,1,128,384]{3,2,1,0:T(8,128)(2,1)} copy(bf16[2,1,128,384]{3,2,1,0:T(8,128)(2,1)} %bitcast.10) | data formatting | bytes 393216
  116.6 0.0 copy-done
  116.7 0.6 copy.13
Async XLA Ops:
  115.0 1.7 %copy-start = (bf16[128,256]{1,0:T(8,128)(2,1)S(1)}, bf16[128,256]{1,0:T(8,128)(2,1)}, u32[]{:S(2)}) copy-start(bf16[128,256]{1,0:T(8,128)(2,1)} %get-tuple-element.7) | copy-start | bytes 196612

commit v4 on v3

--- a/solution.py
+++ b/solution.py
@@ -248,18 +248,15 @@
         dst = window.at[d, span(theirs, i)]
         return remote(dst, dst, side_send.at[d, i], side_recv.at[d, i], {"tok": sibling})
 
+    for hop in (3, 1):
+        for i in range(PIECES):
+
+            @pl.when(chip + hop < chips)
+            def _():
+                up_copy(hop, hop, i).start()
+
     for i in range(PIECES):
         side_copy(0, i).start()
-
-        @pl.when(chip + 1 < chips)
-        def _():
-            up_copy(1, 1, i).start()
-
-    for i in range(PIECES):
-
-        @pl.when(chip + 3 < chips)
-        def _():
-            up_copy(3, 3, i).start()
 
     def own_copy(k):
         to = (place + k) % plane
@@ -352,9 +349,19 @@
             @pl.when((chip >= d) & (d <= reach))
             def _():
                 up_copy(d, hop, i).wait_recv()
+
+            for hop_on in next_hops[:1]:
+
+                @pl.when((chip >= d) & (d + hop_on <= reach) & (chip + hop_on < chips))
+                def _():
+                    up_copy(d + hop_on, hop_on, i).start()
+
+            @pl.when((chip >= d) & (d <= reach))
+            def _():
                 side_copy(d, i).start()
 
-            for hop_on in next_hops:
+        for hop_on in next_hops[1:]:
+            for i in range(PIECES):
 
                 @pl.when((chip >= d) & (d + hop_on <= reach) & (chip + hop_on < chips))
                 def _():
@@ -581,13 +588,16 @@
         near_out[1, v] = parts[1 - core, v].astype(jnp.bfloat16)
         core_copy(v).start()
 
-    def near_copy(k):
+    def groups_of(turn):
+        return pl.ds(2 * ((group // 2 + 1 + turn) % 2), 2)
+
+    def near_copy(k, turn):
         v = (spot + k) % GROUP
         return remote(
-            near_out.at[0, v],
-            near_in.at[GROUP - k],
-            near_send.at[k],
-            near_recv.at[GROUP - k],
+            near_out.at[0, v, groups_of(turn)],
+            near_in.at[GROUP - k, groups_of(turn)],
+            near_send.at[k, turn],
+            near_recv.at[GROUP - k, turn],
             {"tok": near_tok(k)},
         )
 
@@ -599,16 +609,18 @@
             parts[core, v] = total
         else:
             near_out[0, v] = total.astype(jnp.bfloat16)
-            near_copy(k).start()
-
-    def near_arrival(k):
-        return remote(
-            near_out.at[0, spot], near_in.at[k], near_send.at[k], near_recv.at[k], {"tok": tok}
-        )
-
-    for k in range(1, GROUP):
-        near_arrival(k).wait_recv()
-        parts[core, spot] += near_in[k].astype(jnp.float32)
+            near_copy(k, 0).start()
+    for k in (1, 2, 3):
+        near_copy(k, 1).start()
+
+    def near_arrival(k, turn):
+        return remote(
+            near_out.at[0, spot, groups_of(turn)],
+            near_in.at[k, groups_of(turn)],
+            near_send.at[k, turn],
+            near_recv.at[k, turn],
+            {"tok": tok},
+        )
 
     def far_copy(k):
         return remote(
@@ -619,9 +631,15 @@
             {"tok": far_tok(k)},
         )
 
-    for k in range(1, GROUP):
-        far_out[k] = parts[core, spot, (group + k) % GROUP].astype(jnp.bfloat16)
-        far_copy(k).start()
+    odd = group % 2
+    for turn, sent in ((0, (2, 3 - 2 * odd)), (1, (1 + 2 * odd,))):
+        here = groups_of(turn)
+        for k in range(1, GROUP):
+            near_arrival(k, turn).wait_recv()
+            parts[core, spot, here] += near_in[k, here].astype(jnp.float32)
+        for k in sent:
+            far_out[k] = parts[core, spot, (group + k) % GROUP].astype(jnp.bfloat16)
+            far_copy(k).start()
 
     def far_arrival(k):
         return remote(far_out.at[k], far_in.at[k], far_send.at[k], far_recv.at[k], {"tok": tok})
@@ -677,7 +695,8 @@
 
     for k in range(1, GROUP):
         far_copy(k).wait_send()
-        near_copy(k).wait_send()
+        near_copy(k, 0).wait_send()
+        near_copy(k, 1).wait_send()
         grads_copy(k).wait_send()
     for v in range(GROUP):
         core_copy(v).wait_send()
@@ -767,7 +786,9 @@
         + [sems] * 8
         + [dma((16,)), dma((16,)), dma((ranks, SEQS)), dma((2, 2)), dma((2, 2))]
         + [dma((2 + 2 * layers * columns // HD,))]
-        + [dma((4,))] * 8
+        + [dma((4,))] * 4
+        + [dma((4, 2))] * 2
+        + [dma((4,))] * 2
         + [dma((2,))] * 2,
         compiler_params=pltpu.CompilerParams(
             collective_id=0, has_side_effects=True, vmem_limit_bytes=60 * 2**20

time: 118 us -> 115 us (0.975)
  Pallas kernels: 113 us -> 110 us
    pallas_call x1, Pallas kernels: 113 us -> 110 us  [shards(): pl.pallas_call(functools.partial(kernel, n_tok), out_shape=(jax.ShapeDtyp...]
where the time goes in v4:
time: 115 us; the launch traced here: 114 us
  Pallas kernels  110 us (96%)
  local copies, waits for them, and re-layouts  3.78 us (3%)
    pallas_call x1, Pallas kernels, shards(): pl.pallas_call(functools.partial(kernel, n_tok), out_shape=(jax.ShapeDtyp...  110 us
    unnamed x5, local copies, waits for them, and re-layouts  3.78 us

profile of v4, /device:TPU:1, one launch (start us, length us, event | category | flops | bytes accessed | tf_op | source)
XLA Modules:
  0.0 114.3 jit_solution(11887683788636719978)
XLA Ops:
  0.6 109.8 %backward.1 = (bf16[2,128,384]{2,1,0:T(8,128)(2,1)}, bf16[128,256]{1,0:T(8,128)(2,1)}, f32[96,64]{1,0:T(8,128)}) custom-call(s32[4,4]{1,0:T(4,128)} %doc_lens.1, bf16[2,128,384]{2,1,0:T(8,128)(2,1)} %bitcast.8, bf16[2,128,384]{2,1,0:T(8,128)(2,1)} %bitcast.9, bf16[128,256]{1,0:T(8,128)(2,1)} %bitcast.12, bf16[128,384]{1,0:T(8,128)(2,1)} %bitcast.11), custom_call_target="tpu_custom_call" | custom-call | tf_op jit(solution)/shard_map/backward/pallas_call | solution.py:746
  110.5 1.5 %copy.9 = f32[96,64]{0,1:T(8,128)} copy(f32[96,64]{1,0:T(8,128)} %get-tuple-element.11) | data formatting | bytes 49152
  112.0 0.0 copy-start
  112.0 1.7 %copy.12 = bf16[2,1,128,384]{3,2,1,0:T(8,128)(2,1)} copy(bf16[2,1,128,384]{3,2,1,0:T(8,128)(2,1)} %bitcast.10) | data formatting | bytes 393216
  113.6 0.0 copy-done
  113.6 0.6 copy.13
Async XLA Ops:
  112.0 1.7 %copy-start = (bf16[128,256]{1,0:T(8,128)(2,1)S(1)}, bf16[128,256]{1,0:T(8,128)(2,1)}, u32[]{:S(2)}) copy-start(bf16[128,256]{1,0:T(8,128)(2,1)} %get-tuple-element.7) | copy-start | bytes 196612

commit v5 on v4

--- a/solution.py
+++ b/solution.py
@@ -140,11 +140,11 @@
         return half * plane + (place + k) % plane
 
     barrier = pltpu.get_barrier_semaphore()
-    met = [{"tok": sibling}]
+    met = [{"tok": far_tok(k)} for k in range(1, GROUP)]
+    met += [{"hs": leg_hs[0], "tok": opposite}, {"hs": leg_hs[1], "tok": opposite}]
+    met += [{"tok": sibling}]
     met += [{"tok": near_tok(k)} for k in range(1, GROUP)]
-    met += [{"tok": far_tok(k)} for k in range(1, GROUP)]
     met += [{"hs": plane_hs(k)} for k in range(1, plane)]
-    met += [{"hs": leg_hs[0], "tok": opposite}, {"hs": leg_hs[1], "tok": opposite}]
     met += [{"hs": beside, "tok": sibling}]
     expected = len(met)
     for k in (1, 3):
@@ -397,9 +397,6 @@
         stats_block(d + 2)
         joined(d + 3)
 
-    leg_copy(0, 1).wait_recv()
-    leg_copy(1, 1).start()
-
     inverse = 1.0 / row_total[...]
     row_delta = stats.at[3:4]
     row_delta[...] = row_weighted[...] * inverse
@@ -483,9 +480,15 @@
         d = 3 * (reach // 3 - turn)
         grads_block(d + 2)
         grads_block(d + 1)
+
+        @pl.when(turn == 0)
+        def _():
+            leg_copy(0, 1).wait_recv()
+            leg_copy(1, 1).start()
+
+        sent_down(d + 6, 3, (1, 3))
         sent_down(d + 4, 1, (1,))
         sent_down(d + 2, 1, ())
-        sent_down(d + 6, 3, (1, 3))
         grads_block(d)
 
         @pl.when(turn == 1)
@@ -500,9 +503,6 @@
             query_grads[layer, :, head * HD : (head + 1) * HD] = block.astype(jnp.bfloat16)
     sent_down(1, 1, (1,))
     sent_down(3, 3, (1, 3))
-    leg_copy(1, 1).wait_recv()
-    spread(1)
-    feat_all[other_rank, x] = feat_cross[x % 2]
     for i in range(PIECES):
         summed(0, i, (1, 3))
 
@@ -534,6 +534,9 @@
     for k in range(1, SEQS):
         grads_copy(k).start()
     grads_in[pl.ds(pl.multiple_of(x * rows, rows), rows)] = grads_out[x // 2]
+    leg_copy(1, 1).wait_recv()
+    spread(1)
+    feat_all[other_rank, x] = feat_cross[x % 2]
 
     def feat_arrival(from_rank, k):
         came = (place + k) % plane

time: 115 us -> 121 us (1.052)
  Pallas kernels: 110 us -> 117 us
    pallas_call x1, Pallas kernels: 110 us -> 117 us  [shards(): pl.pallas_call(functools.partial(kernel, n_tok), out_shape=(jax.ShapeDtyp...]
where the time goes in v5:
time: 121 us
  Pallas kernels  117 us (97%)
  local copies, waits for them, and re-layouts  3.78 us (3%)
    pallas_call x1, Pallas kernels, shards(): pl.pallas_call(functools.partial(kernel, n_tok), out_shape=(jax.ShapeDtyp...  117 us
    unnamed x5, local copies, waits for them, and re-layouts  3.78 us

profile of v5, /device:TPU:1, one launch (start us, length us, event | category | flops | bytes accessed | tf_op | source)
XLA Modules:
  0.0 121.1 jit_solution(14803008093699821419)
XLA Ops:
  0.6 116.7 %backward.1 = (bf16[2,128,384]{2,1,0:T(8,128)(2,1)}, bf16[128,256]{1,0:T(8,128)(2,1)}, f32[96,64]{1,0:T(8,128)}) custom-call(s32[4,4]{1,0:T(4,128)} %doc_lens.1, bf16[2,128,384]{2,1,0:T(8,128)(2,1)} %bitcast.8, bf16[2,128,384]{2,1,0:T(8,128)(2,1)} %bitcast.9, bf16[128,256]{1,0:T(8,128)(2,1)} %bitcast.12, bf16[128,384]{1,0:T(8,128)(2,1)} %bitcast.11), custom_call_target="tpu_custom_call" | custom-call | tf_op jit(solution)/shard_map/backward/pallas_call | solution.py:749
  117.3 1.5 %copy.9 = f32[96,64]{0,1:T(8,128)} copy(f32[96,64]{1,0:T(8,128)} %get-tuple-element.11) | data formatting | bytes 49152
  118.8 0.0 copy-start
  118.8 1.7 %copy.12 = bf16[2,1,128,384]{3,2,1,0:T(8,128)(2,1)} copy(bf16[2,1,128,384]{3,2,1,0:T(8,128)(2,1)} %bitcast.10) | data formatting | bytes 393216
  120.5 0.0 copy-done
  120.5 0.6 copy.13
Async XLA Ops:
  118.8 1.7 %copy-start = (bf16[128,256]{1,0:T(8,128)(2,1)S(1)}, bf16[128,256]{1,0:T(8,128)(2,1)}, u32[]{:S(2)}) copy-start(bf16[128,256]{1,0:T(8,128)(2,1)} %get-tuple-element.7) | copy-start | bytes 196612
